TPU v7x, 512 devices: a whole 4x8x8 slice. The times are simulated.
512 devices in a mesh: seq: 64 (over y, x, core), head: 8 (over z).
Axes of the slice: x: 4, y: 8, z: 8, core: 2. Of those that a mesh axis runs over, the one named last changes fastest.
Arguments:
- x_proj: bfloat16 [8192, 8192], P(('seq', 'head')), may hold values from -6 to 6
- z_gate: bfloat16 [8192, 8192], P(('seq', 'head')), may hold values from -6 to 6
- out_grad: bfloat16 [8192, 8192], P(('seq', 'head')), may hold values from -6 to 6
- b_proj: bfloat16 [8192, 1024], P(('seq', 'head')), may hold values from -1 to 1
- c_proj: bfloat16 [8192, 1024], P(('seq', 'head')), may hold values from -1 to 1
- dt_raw: bfloat16 [8192, 128], P(('seq', 'head')), may hold values from -3 to 3
- dt_bias: float32 [128], P('head'), may hold values from -0.5 to 0.5
- a_log: float32 [128], P('head')
- d_skip: float32 [128], P('head'), may hold values from 0.5 to 1.5
Outputs:
- grad_x: bfloat16 [8192, 8192], P(('seq', 'head'))
- grad_z: bfloat16 [8192, 8192], P(('seq', 'head'))
- grad_b: bfloat16 [8192, 1024], P(('seq', 'head'))
- grad_c: bfloat16 [8192, 1024], P(('seq', 'head'))
- grad_dt: bfloat16 [8192, 128], P(('seq', 'head'))
- grad_bias: float32 [128], P('head')
- grad_alog: float32 [128], P('head')
- grad_dskip: float32 [128], P('head')
All inputs are finite; a program needn't handle non-finite values.
Results may differ from a plain program's by a relative error of at most 0.0103.
Values may be sent and summed in bfloat16 or wider, within the bound.
A program may use at most 192 MiB of HBM per device.

v0:
```python
import jax
import jax.numpy as jnp
from jax import lax
from jax.sharding import PartitionSpec as P

HEADS = 128
HEAD_DIM = 64
STATE = 128
GROUPS = 8
BLOCK = 32


PRECISE = lax.Precision.HIGHEST


def prefix(array, axis, combine, identity, reverse):
    size, place = (lax.axis_size(axis), lax.axis_index(axis))
    everything = jax.tree.map(lambda part: lax.all_gather(part, axis), array)
    start = jax.tree.map(
        lambda part, zero: jnp.broadcast_to(jnp.asarray(zero, part.dtype), part.shape),
        array,
        identity,
    )

    def turn(k, before):
        at = size - 1 - k if reverse else k
        reached = at > place if reverse else at < place
        new = combine(before, jax.tree.map(lambda part: part[at], everything))
        return jax.tree.map(lambda a, b: jnp.where(reached, a, b), new, before)

    return lax.fori_loop(0, size, turn, start)


def block_forward(
    x_heads, b_heads, c_heads, raw_steps, step_bias, decay_log, skip_gain, carry_state
):
    step_size = jax.nn.softplus(raw_steps + step_bias)
    cumlog = jnp.cumsum(-jnp.exp(decay_log) * step_size, axis=0)
    across = jnp.transpose(cumlog, (1, 2, 0))
    step_cols = jnp.transpose(step_size, (1, 2, 0))
    length = x_heads.shape[0]
    positions = jnp.arange(length)
    causal = positions[:, None] >= positions[None, :]
    spread = jnp.where(causal[None, None], across[:, :, :, None] - across[:, :, None, :], -jnp.inf)
    affinity = jnp.einsum("tgn,sgn->gts", c_heads, b_heads, precision=PRECISE)
    scores = jnp.exp(spread) * affinity[:, None] * step_cols[:, :, None, :]
    output = jnp.einsum("gjts,sgjp->tgjp", scores, x_heads, precision=PRECISE)
    carried = jnp.einsum("tgn,gjpn->tgjp", c_heads, carry_state, precision=PRECISE)
    output = output + jnp.exp(cumlog)[..., None] * carried
    output = output + skip_gain[..., None] * x_heads
    weights = jnp.exp(cumlog[-1][None] - cumlog) * step_size
    ending = jnp.einsum("tgn,tgjp->gjpn", b_heads, weights[..., None] * x_heads, precision=PRECISE)
    ending = ending + jnp.exp(cumlog[-1])[..., None, None] * carry_state
    return (output, ending)


def silu_slope(signal):
    squash = jax.nn.sigmoid(signal)
    return squash * (1.0 + signal * (1.0 - squash))


def combine_carry(earlier, latter):
    return (earlier[0] * latter[0], latter[0][..., None, None] * earlier[1] + latter[1])


def shards(x_proj, z_gate, out_grad, b_proj, c_proj, dt_raw, dt_bias, a_log, d_skip):
    head_ways = lax.axis_size("head")
    groups_here = GROUPS // head_ways
    per_group = HEADS // GROUPS
    x_local, z_local, cot_local, b_local, c_local, raw_local = (
        lax.all_to_all(x_proj, "head", split_axis=1, concat_axis=0, tiled=True),
        lax.all_to_all(z_gate, "head", split_axis=1, concat_axis=0, tiled=True),
        lax.all_to_all(out_grad, "head", split_axis=1, concat_axis=0, tiled=True),
        lax.all_to_all(b_proj, "head", split_axis=1, concat_axis=0, tiled=True),
        lax.all_to_all(c_proj, "head", split_axis=1, concat_axis=0, tiled=True),
        lax.all_to_all(dt_raw, "head", split_axis=1, concat_axis=0, tiled=True),
    )
    gated = (cot_local.astype(jnp.float32) * jax.nn.silu(z_local.astype(jnp.float32))).astype(
        jnp.bfloat16
    )
    length = x_local.shape[0]
    sections = length // BLOCK
    x_heads = x_local.astype(jnp.float32).reshape(length, groups_here, per_group, HEAD_DIM)
    gated_heads = gated.astype(jnp.float32).reshape(length, groups_here, per_group, HEAD_DIM)
    b_heads = b_local.astype(jnp.float32).reshape(length, groups_here, STATE)
    c_heads = c_local.astype(jnp.float32).reshape(length, groups_here, STATE)
    raw_steps = raw_local.astype(jnp.float32).reshape(length, groups_here, per_group)
    step_bias = dt_bias.reshape(groups_here, per_group)
    decay_log = a_log.reshape(groups_here, per_group)
    skip_gain = d_skip.reshape(groups_here, per_group)
    step_size = jax.nn.softplus(raw_steps + step_bias)
    cumlog = jnp.cumsum(-jnp.exp(decay_log) * step_size, axis=0)
    keep_factor = jnp.exp(cumlog[-1])
    weights = jnp.exp(cumlog[-1][None] - cumlog) * step_size
    local_state = jnp.einsum(
        "tgn,tgjp->gjpn", b_heads, weights[..., None] * x_heads, precision=PRECISE
    )
    identity = (jnp.ones_like(keep_factor), jnp.zeros_like(local_state))
    incoming = prefix((keep_factor, local_state), "seq", combine_carry, identity, False)[1]
    reach_decay = jnp.exp(cumlog)
    local_adjoint = jnp.einsum(
        "tgn,tgjp->gjpn", c_heads, reach_decay[..., None] * gated_heads, precision=PRECISE
    )
    identity = (jnp.ones_like(keep_factor), jnp.zeros_like(local_adjoint))
    returning = prefix((keep_factor, local_adjoint), "seq", combine_carry, identity, True)[1]

    def local_slab(x_in, b_in, c_in, raw_in, bias_in, alog_in, skip_in):

        def advance(carry_state, section):
            x_sec, b_sec, c_sec, raw_sec = section
            result, next_state = block_forward(
                x_sec, b_sec, c_sec, raw_sec, bias_in, alog_in, skip_in, carry_state
            )
            return (next_state, result)

        sections_in = (
            x_in.reshape(sections, BLOCK, groups_here, per_group, HEAD_DIM),
            b_in.reshape(sections, BLOCK, groups_here, STATE),
            c_in.reshape(sections, BLOCK, groups_here, STATE),
            raw_in.reshape(sections, BLOCK, groups_here, per_group),
        )
        final_state, results = lax.scan(advance, incoming, sections_in)
        return (results.reshape(length, groups_here, per_group, HEAD_DIM), final_state)

    primal, pullback = jax.vjp(
        local_slab, x_heads, b_heads, c_heads, raw_steps, step_bias, decay_log, skip_gain
    )
    gradients = pullback((gated_heads, returning))
    saved_out = primal[0].astype(jnp.bfloat16).reshape(length, -1)
    restored = lax.optimization_barrier(saved_out).astype(jnp.float32)
    z_values = z_local.astype(jnp.float32)
    second = (cot_local.astype(jnp.float32) * restored * silu_slope(z_values)).astype(jnp.bfloat16)
    grad_x, second_tokens, grad_b, grad_c, grad_dt = (
        lax.all_to_all(
            gradients[0].astype(jnp.bfloat16).reshape(length, -1),
            "head",
            split_axis=0,
            concat_axis=1,
            tiled=True,
        ),
        lax.all_to_all(second, "head", split_axis=0, concat_axis=1, tiled=True),
        lax.all_to_all(
            gradients[1].astype(jnp.bfloat16).reshape(length, -1),
            "head",
            split_axis=0,
            concat_axis=1,
            tiled=True,
        ),
        lax.all_to_all(
            gradients[2].astype(jnp.bfloat16).reshape(length, -1),
            "head",
            split_axis=0,
            concat_axis=1,
            tiled=True,
        ),
        lax.all_to_all(
            gradients[3].astype(jnp.bfloat16).reshape(length, -1),
            "head",
            split_axis=0,
            concat_axis=1,
            tiled=True,
        ),
    )
    totals = lax.psum(
        (gradients[4].reshape(-1), gradients[5].reshape(-1), gradients[6].reshape(-1)), "seq"
    )
    return (grad_x, second_tokens, grad_b, grad_c, grad_dt, totals[0], totals[1], totals[2])


def solution(mesh):
    placed = (
        P(("seq", "head"), None),
        P(("seq", "head"), None),
        P(("seq", "head"), None),
        P(("seq", "head"), None),
        P(("seq", "head"), None),
        P(("seq", "head"), None),
        P("head"),
        P("head"),
        P("head"),
    )
    return jax.shard_map(
        shards,
        mesh=mesh,
        in_specs=placed,
        out_specs=(
            P(("seq", "head"), None),
            P(("seq", "head"), None),
            P(("seq", "head"), None),
            P(("seq", "head"), None),
            P(("seq", "head"), None),
            P("head"),
            P("head"),
            P("head"),
        ),
        check_vma=False,
    )
```

profile of v0, /device:TPU:1, one launch (start us, length us, event | category | flops | bytes accessed | tf_op | source)
XLA Modules:
  0.0 798.8 jit_solution(10307650940229109779)
XLA Ops:
  8.7 10.9 %all-to-all-start = ((bf16[8,2,128]{2,1,0:T(2,128)(2,1)}), bf16[8,2,128]{2,1,0:T(2,128)(2,1)S(1)}, u32[]{:S(2)}, u32[]{:S(2)}) async-start(bf16[8,2,128]{2,1,0:T(2,128)(2,1)} %reshape.1760), calls=%async_computation | async-start | bytes 8192 | tf_op jit(solution)/shard_map/all_to_all | solution.py:76
  21.8 4.2 all-to-all-done
  26.0 3.4 all-to-all-start.2
  33.4 5.3 all-to-all-done.2
  38.6 3.4 all-to-all-start.1
  43.6 7.8 all-to-all-done.1
  51.5 3.3 all-to-all-start.3
  55.3 6.3 all-to-all-done.3
  61.6 1.9 fusion.123
  64.2 3.4 all-to-all-start.4
  69.0 8.0 all-to-all-done.4
  76.9 3.3 all-to-all-start.5
  80.7 6.4 all-to-all-done.5
  87.1 1.9 fusion.121
  91.9 44.3 %all_gather.18 = f32[64,1,16]{2,1,0:T(1,128)S(1)} all-gather(f32[1,1,16]{2,1,0:T(1,128)S(1)} %get-tuple-element.2184), channel_id=1, replica_groups=mesh['seq'=64,'head'=8] {'seq'}, dimensions={0}, use_global_device_ids=true | all-gather | bytes 4160 | tf_op jit(solution)/shard_map/all_gather | solution.py:18
  143.0 1.8 fusion.132
  144.9 68.2 %all-gather.5.cloned.1.call-done = f32[1024,64,128]{2,1,0:T(8,128)} async-done(((f32[16,64,128]{2,1,0:T(8,128)}), f32[1024,64,128]{2,1,0:T(8,128)}) %all-gather.5.cloned.1.call-update) | async-done | bytes 33554448 | tf_op jit(solution)/shard_map/all_gather | solution.py:18
  213.1 78.9 %while.112 = (s32[]{:T(128)}, f32[1,16,64,128]{3,2,1,0:T(8,128)S(1)}, s32[]{:T(128)}, f32[64,1,16]{2,1,0:T(1,128)S(1)}, f32[64,1,16,64,128]{4,3,2,1,0:T(8,128)}) while((s32[]{:T(128)}, f32[1,16,64,128]{3,2,1,0:T(8,128)S(1)}, s32[]{:T(128)}, f32[64,1,16]{2,1,0:T(1,128)S(1)}, f32[64,1,16,64,128]{4,3,2,1,0:T(8,128)}) %tuple.272), condition=%wide.region_2.3_spmd.clone.clone, body=%wide.region_1.2_spmd.clone.sunk.clone | while | flops 524296 | bytes 1573199 | solution.py:31
  292.0 69.5 %all-gather.7.cloned.1.call-done = f32[1024,64,128]{2,1,0:T(8,128)} async-done(((f32[16,64,128]{2,1,0:T(8,128)}), f32[1024,64,128]{2,1,0:T(8,128)}) %all-gather.7.cloned.1.call-update) | async-done | bytes 33554448 | tf_op jit(solution)/shard_map/all_gather | solution.py:18
  361.4 77.7 %while.113 = (s32[]{:T(128)}, f32[1,16,64,128]{3,2,1,0:T(8,128)S(1)}, s32[]{:T(128)}, f32[64,1,16]{2,1,0:T(1,128)S(1)}, f32[64,1,16,64,128]{4,3,2,1,0:T(8,128)}) while((s32[]{:T(128)}, f32[1,16,64,128]{3,2,1,0:T(8,128)S(1)}, s32[]{:T(128)}, f32[64,1,16]{2,1,0:T(1,128)S(1)}, f32[64,1,16,64,128]{4,3,2,1,0:T(8,128)}) %tuple.273), condition=%wide.region_4.5_spmd.clone.clone, body=%wide.region_3.4_spmd.clone.sunk.clone | while | flops 524292 | bytes 1573153 | solution.py:31
  442.1 88.6 %while.111 = (s32[]{:T(128)}, f32[1,16,64,128]{3,2,1,0:T(8,128)S(1)}, bf16[4,32,1,16,64]{4,1,3,2,0:T(8,128)(2,1)}, f32[4,32,1,16]{1,3,2,0:T(8,128)}, f32[4,32,1,...) while((s32[]{:T(128)}, ...), condition=%wide.region_7.8_spmd.clone.clone.clone, body=%wide.region_5.7_spmd.clone.clone.sunk.clone | while | flops 115448320 | bytes 5851961 | solution.py:122
  442.9 2.2 bitcast_dynamic-update-slice_fusion.15
  449.5 1.9 fusion.245
  453.7 1.8 fusion.246
  465.1 2.2 bitcast_dynamic-update-slice_fusion.15
  471.6 1.9 fusion.245
  475.8 1.9 fusion.246
  479.7 1.8 multiply_dynamic-update-slice_fusion.6
  487.2 2.2 bitcast_dynamic-update-slice_fusion.15
  493.8 1.9 fusion.245
  498.0 1.8 fusion.246
  501.9 1.8 multiply_dynamic-update-slice_fusion.6
  509.4 2.2 bitcast_dynamic-update-slice_fusion.15
  516.0 1.9 fusion.245
  520.2 1.9 fusion.246
  531.4 78.2 %while.114 = (s32[]{:T(128)}, f32[1,16]{1,0:T(1,128)}, f32[1,16]{1,0:T(1,128)}, f32[1,16]{1,0:T(1,128)}, f32[1,16,64,128]{3,2,1,0:T(8,128)S(1)}, /*index=5*/bf16...) while((s32[]{:T(128)}, f32[1,16]{1,0:T(1,128)}, ...), condition=%wide.region_21.22_spmd.clone.clone, body=%wide.region_8.21_spmd.clone.sunk.clone | while | flops 230750784 | bytes 9777600 | solution.py:122
  531.4 2.6 fusion.264
  551.0 2.6 fusion.264
  570.6 2.6 fusion.264
  590.2 2.6 fusion.264
  610.6 13.4 %all_to_all.167 = bf16[8,2,128]{2,1,0:T(2,128)(2,1)S(1)} all-to-all(bf16[8,2,128]{2,1,0:T(2,128)(2,1)S(1)} %reshape.1762), channel_id=1, replica_groups=mesh['seq'=64,'head'=8] {'head'}, dimensions={0} | all-to-all | bytes 8192 | tf_op jit(solution)/shard_map/all_to_all | solution.py:156
  624.0 9.2 %all_to_all.168 = bf16[8,16,128]{2,1,0:T(8,128)(2,1)S(1)} all-to-all(bf16[8,16,128]{2,1,0:T(8,128)(2,1)S(1)} %bitcast.772), channel_id=1, replica_groups=mesh['seq'=64,'head'=8] {'head'}, dimensions={0} | all-to-all | bytes 65536 | tf_op jit(solution)/shard_map/all_to_all | solution.py:142
  633.2 3.3 all-to-all-start.9
  638.9 4.4 all-to-all-done.9
  643.3 3.4 all-to-all-start.6
  648.3 7.7 all-to-all-done.6
  656.0 3.4 all-to-all-start.7
  659.5 129.0 %all-reduce.2 = (f32[16]{0:T(128)}, f32[16]{0:T(128)}, f32[16]{0:T(128)}) all-reduce(f32[16]{0:T(128)S(1)} %bitcast.777, f32[16]{0:T(128)S(1)} %bitcast.778, f32[16]{0:T(128)S(1)} %bitcast.776), channel_id=1, replica_groups=mesh['seq'=64,'head'=8] {'seq'}, use_global_device_ids=true, to_apply=%region_22.23 | all-reduce | flops 48 | bytes 384 | tf_op jit(solution)/shard_map/psum | solution.py:164
  (698 shorter events, 313.2 us)
Async XLA Ops:
  7.2 12.4 %copy-start = (bf16[16,1024]{1,0:T(8,128)(2,1)S(1)}, bf16[16,1024]{1,0:T(8,128)(2,1)}, u32[]{:S(2)}) copy-start(bf16[16,1024]{1,0:T(8,128)(2,1)} %param.21) | copy-start | bytes 98308
  8.7 17.3 %all-to-all-start = ((bf16[8,2,128]{2,1,0:T(2,128)(2,1)}), bf16[8,2,128]{2,1,0:T(2,128)(2,1)S(1)}, u32[]{:S(2)}, u32[]{:S(2)}) async-start(bf16[8,2,128]{2,1,0:T(2,128)(2,1)} %reshape.1760), calls=%async_computation | async-start | bytes 8192 | tf_op jit(solution)/shard_map/all_to_all | solution.py:76
  26.0 12.6 %all-to-all-start.2 = ((bf16[16,8,1024]{2,0,1:T(8,128)(2,1)}), bf16[16,8,1024]{2,0,1:T(8,128)(2,1)S(1)}, u32[]{:S(2)}, u32[]{:S(2)}) async-start(bf16[16,8,1024]{2,0,1:T(8,128)(2,1)} %bitcast.485), calls=%async_computation.2 | async-start | bytes 524288 | tf_op jit(solution)/shard_map/all_to_all | solution.py:72
  38.6 103.1 %copy-start.5 = (bf16[16,8,1024]{2,0,1:T(8,128)(2,1)}, bf16[16,8,1024]{2,0,1:T(8,128)(2,1)S(1)}, u32[]{:S(2)}) copy-start(bf16[16,8,1024]{2,0,1:T(8,128)(2,1)S(1)} %all-to-all-done.2) | copy-start | bytes 786436
  38.6 12.9 %all-to-all-start.1 = ((bf16[16,8,1024]{2,0,1:T(8,128)(2,1)}), bf16[16,8,1024]{2,0,1:T(8,128)(2,1)S(1)}, u32[]{:S(2)}, u32[]{:S(2)}) async-start(bf16[16,8,1024]{2,0,1:T(8,128)(2,1)} %bitcast.486), calls=%async_computation.1 | async-start | bytes 524288 | tf_op jit(solution)/shard_map/all_to_all | solution.py:73
  51.5 12.0 %copy-start.7 = (bf16[16,8,1024]{2,0,1:T(8,128)(2,1)}, bf16[16,8,1024]{2,0,1:T(8,128)(2,1)S(1)}, u32[]{:S(2)}) copy-start(bf16[16,8,1024]{2,0,1:T(8,128)(2,1)S(1)} %all-to-all-done.1) | copy-start | bytes 786436
  51.5 10.1 %all-to-all-start.3 = ((bf16[16,8,128]{2,0,1:T(8,128)(2,1)}), bf16[16,8,128]{2,0,1:T(8,128)(2,1)S(1)}, u32[]{:S(2)}, u32[]{:S(2)}) async-start(bf16[16,8,128]{2,0,1:T(8,128)(2,1)} %copy_bitcast_fusion.6), calls=%async_computation.3 | async-start | bytes 65536 | tf_op jit(solution)/shard_map/all_to_all | solution.py:75
  54.8 158.3 %all-gather.5.cloned.1.call-start = ((), (), s32[]{:S(2)}) async-start(), calls=%async_computation.11 | async-start | bytes 34078720 | tf_op jit(solution)/shard_map/all_gather | solution.py:18
  55.1 12.6 %copy-start.17 = (bf16[16,1024]{1,0:T(8,128)(2,1)S(1)}, bf16[16,1024]{1,0:T(8,128)(2,1)}, u32[]{:S(2)}) copy-start(bf16[16,1024]{1,0:T(8,128)(2,1)} %param.20) | copy-start | bytes 98308
  64.2 12.7 %all-to-all-start.4 = ((bf16[16,8,1024]{2,0,1:T(8,128)(2,1)}), bf16[16,8,1024]{2,0,1:T(8,128)(2,1)S(1)}, u32[]{:S(2)}, u32[]{:S(2)}) async-start(bf16[16,8,1024]{2,0,1:T(8,128)(2,1)} %bitcast.484), calls=%async_computation.4 | async-start | bytes 524288 | tf_op jit(solution)/shard_map/all_to_all | solution.py:71
  76.9 10.1 %all-to-all-start.5 = ((bf16[16,8,128]{2,0,1:T(8,128)(2,1)}), bf16[16,8,128]{2,0,1:T(8,128)(2,1)S(1)}, u32[]{:S(2)}, u32[]{:S(2)}) async-start(bf16[16,8,128]{2,0,1:T(8,128)(2,1)} %copy_bitcast_fusion.5), calls=%async_computation.5 | async-start | bytes 65536 | tf_op jit(solution)/shard_map/all_to_all | solution.py:74
  80.3 281.1 %all-gather.7.cloned.1.call-start = ((), (), s32[]{:S(2)}) async-start(), calls=%async_computation.12 | async-start | bytes 34078720 | tf_op jit(solution)/shard_map/all_gather | solution.py:18
  89.2 48.5 %copy-start.2 = (bf16[4,32,1,16,64]{4,1,3,2,0:T(8,128)(2,1)}, bf16[4,32,1,16,64]{4,1,3,2,0:T(8,128)(2,1)S(1)}, u32[]{:S(2)}) copy-start(bf16[4,32,1,16,64]{4,1,3,2,0:T(8,128)(2,1)S(1)} %fusion.139) | copy-start | bytes 786436
  531.4 9.2 %copy-start.15 = (bf16[4,32,1,16]{1,3,2,0:T(8,128)(2,1)S(1)}, bf16[4,32,1,16]{1,3,2,0:T(8,128)(2,1)}, u32[]{:S(2)}) copy-start(bf16[4,32,1,16]{1,3,2,0:T(8,128)(2,1)} %get-tuple-element.3027) | copy-start | bytes 12292 | tf_op jit(solution)/shard_map/transpose(jvp())/while
  531.4 10.2 %copy-start.18 = (f32[1,16]{1,0:T(1,128)S(1)}, f32[1,16]{1,0:T(1,128)}, u32[]{:S(2)}) copy-start(f32[1,16]{1,0:T(1,128)} %get-tuple-element.3076) | copy-start | bytes 196 | tf_op jit(solution)/shard_map/transpose(jvp())/while
  531.4 10.2 %copy-start.22 = (f32[1,16]{1,0:T(1,128)S(1)}, f32[1,16]{1,0:T(1,128)}, u32[]{:S(2)}) copy-start(f32[1,16]{1,0:T(1,128)} %get-tuple-element.3020) | copy-start | bytes 196 | tf_op jit(solution)/shard_map/transpose(jvp())/while
  531.4 10.2 %copy-start.25 = (f32[1,16]{1,0:T(1,128)S(1)}, f32[1,16]{1,0:T(1,128)}, u32[]{:S(2)}) copy-start(f32[1,16]{1,0:T(1,128)} %get-tuple-element.3021) | copy-start | bytes 196 | tf_op jit(solution)/shard_map/transpose(jvp())/while
  531.4 10.3 %copy-start.19 = (f32[1,16]{1,0:T(1,128)S(1)}, f32[1,16]{1,0:T(1,128)}, u32[]{:S(2)}) copy-start(f32[1,16]{1,0:T(1,128)} %get-tuple-element.3022) | copy-start | bytes 196 | tf_op jit(solution)/shard_map/transpose(jvp())/while
  541.4 9.5 %copy-start.16 = (bf16[4,32,1,16]{1,3,2,0:T(8,128)(2,1)}, bf16[4,32,1,16]{1,3,2,0:T(8,128)(2,1)S(1)}, u32[]{:S(2)}) copy-start(bf16[4,32,1,16]{1,3,2,0:T(8,128)(2,1)S(1)} %get-tuple-element.3060) | copy-start | bytes 12292 | tf_op jit(solution)/shard_map/transpose(jvp())/while
  541.7 9.2 %copy-start.23 = (f32[1,16]{1,0:T(1,128)}, f32[1,16]{1,0:T(1,128)S(1)}, u32[]{:S(2)}) copy-start(f32[1,16]{1,0:T(1,128)S(1)} %get-tuple-element.3053) | copy-start | bytes 196 | tf_op jit(solution)/shard_map/transpose(jvp())/while
  551.0 9.2 %copy-start.15 = (bf16[4,32,1,16]{1,3,2,0:T(8,128)(2,1)S(1)}, bf16[4,32,1,16]{1,3,2,0:T(8,128)(2,1)}, u32[]{:S(2)}) copy-start(bf16[4,32,1,16]{1,3,2,0:T(8,128)(2,1)} %get-tuple-element.3027) | copy-start | bytes 12292 | tf_op jit(solution)/shard_map/transpose(jvp())/while
  551.0 10.2 %copy-start.18 = (f32[1,16]{1,0:T(1,128)S(1)}, f32[1,16]{1,0:T(1,128)}, u32[]{:S(2)}) copy-start(f32[1,16]{1,0:T(1,128)} %get-tuple-element.3076) | copy-start | bytes 196 | tf_op jit(solution)/shard_map/transpose(jvp())/while
  551.0 10.2 %copy-start.22 = (f32[1,16]{1,0:T(1,128)S(1)}, f32[1,16]{1,0:T(1,128)}, u32[]{:S(2)}) copy-start(f32[1,16]{1,0:T(1,128)} %get-tuple-element.3020) | copy-start | bytes 196 | tf_op jit(solution)/shard_map/transpose(jvp())/while
  551.0 10.2 %copy-start.25 = (f32[1,16]{1,0:T(1,128)S(1)}, f32[1,16]{1,0:T(1,128)}, u32[]{:S(2)}) copy-start(f32[1,16]{1,0:T(1,128)} %get-tuple-element.3021) | copy-start | bytes 196 | tf_op jit(solution)/shard_map/transpose(jvp())/while
  551.0 10.3 %copy-start.19 = (f32[1,16]{1,0:T(1,128)S(1)}, f32[1,16]{1,0:T(1,128)}, u32[]{:S(2)}) copy-start(f32[1,16]{1,0:T(1,128)} %get-tuple-element.3022) | copy-start | bytes 196 | tf_op jit(solution)/shard_map/transpose(jvp())/while
  561.0 9.5 %copy-start.16 = (bf16[4,32,1,16]{1,3,2,0:T(8,128)(2,1)}, bf16[4,32,1,16]{1,3,2,0:T(8,128)(2,1)S(1)}, u32[]{:S(2)}) copy-start(bf16[4,32,1,16]{1,3,2,0:T(8,128)(2,1)S(1)} %get-tuple-element.3060) | copy-start | bytes 12292 | tf_op jit(solution)/shard_map/transpose(jvp())/while
  561.2 9.2 %copy-start.23 = (f32[1,16]{1,0:T(1,128)}, f32[1,16]{1,0:T(1,128)S(1)}, u32[]{:S(2)}) copy-start(f32[1,16]{1,0:T(1,128)S(1)} %get-tuple-element.3053) | copy-start | bytes 196 | tf_op jit(solution)/shard_map/transpose(jvp())/while
  561.3 9.2 %copy-start.26 = (f32[1,16]{1,0:T(1,128)}, f32[1,16]{1,0:T(1,128)S(1)}, u32[]{:S(2)}) copy-start(f32[1,16]{1,0:T(1,128)S(1)} %get-tuple-element.3054) | copy-start | bytes 196 | tf_op jit(solution)/shard_map/transpose(jvp())/while
  570.6 10.2 %copy-start.18 = (f32[1,16]{1,0:T(1,128)S(1)}, f32[1,16]{1,0:T(1,128)}, u32[]{:S(2)}) copy-start(f32[1,16]{1,0:T(1,128)} %get-tuple-element.3076) | copy-start | bytes 196 | tf_op jit(solution)/shard_map/transpose(jvp())/while
  570.6 10.2 %copy-start.22 = (f32[1,16]{1,0:T(1,128)S(1)}, f32[1,16]{1,0:T(1,128)}, u32[]{:S(2)}) copy-start(f32[1,16]{1,0:T(1,128)} %get-tuple-element.3020) | copy-start | bytes 196 | tf_op jit(solution)/shard_map/transpose(jvp())/while
  570.6 10.2 %copy-start.25 = (f32[1,16]{1,0:T(1,128)S(1)}, f32[1,16]{1,0:T(1,128)}, u32[]{:S(2)}) copy-start(f32[1,16]{1,0:T(1,128)} %get-tuple-element.3021) | copy-start | bytes 196 | tf_op jit(solution)/shard_map/transpose(jvp())/while
  570.6 10.2 %copy-start.19 = (f32[1,16]{1,0:T(1,128)S(1)}, f32[1,16]{1,0:T(1,128)}, u32[]{:S(2)}) copy-start(f32[1,16]{1,0:T(1,128)} %get-tuple-element.3022) | copy-start | bytes 196 | tf_op jit(solution)/shard_map/transpose(jvp())/while
  580.5 9.5 %copy-start.16 = (bf16[4,32,1,16]{1,3,2,0:T(8,128)(2,1)}, bf16[4,32,1,16]{1,3,2,0:T(8,128)(2,1)S(1)}, u32[]{:S(2)}) copy-start(bf16[4,32,1,16]{1,3,2,0:T(8,128)(2,1)S(1)} %get-tuple-element.3060) | copy-start | bytes 12292 | tf_op jit(solution)/shard_map/transpose(jvp())/while
  590.1 10.2 %copy-start.18 = (f32[1,16]{1,0:T(1,128)S(1)}, f32[1,16]{1,0:T(1,128)}, u32[]{:S(2)}) copy-start(f32[1,16]{1,0:T(1,128)} %get-tuple-element.3076) | copy-start | bytes 196 | tf_op jit(solution)/shard_map/transpose(jvp())/while
  590.1 10.2 %copy-start.22 = (f32[1,16]{1,0:T(1,128)S(1)}, f32[1,16]{1,0:T(1,128)}, u32[]{:S(2)}) copy-start(f32[1,16]{1,0:T(1,128)} %get-tuple-element.3020) | copy-start | bytes 196 | tf_op jit(solution)/shard_map/transpose(jvp())/while
  590.1 10.2 %copy-start.25 = (f32[1,16]{1,0:T(1,128)S(1)}, f32[1,16]{1,0:T(1,128)}, u32[]{:S(2)}) copy-start(f32[1,16]{1,0:T(1,128)} %get-tuple-element.3021) | copy-start | bytes 196 | tf_op jit(solution)/shard_map/transpose(jvp())/while
  590.2 10.2 %copy-start.19 = (f32[1,16]{1,0:T(1,128)S(1)}, f32[1,16]{1,0:T(1,128)}, u32[]{:S(2)}) copy-start(f32[1,16]{1,0:T(1,128)} %get-tuple-element.3022) | copy-start | bytes 196 | tf_op jit(solution)/shard_map/transpose(jvp())/while
  600.1 9.5 %copy-start.16 = (bf16[4,32,1,16]{1,3,2,0:T(8,128)(2,1)}, bf16[4,32,1,16]{1,3,2,0:T(8,128)(2,1)S(1)}, u32[]{:S(2)}) copy-start(bf16[4,32,1,16]{1,3,2,0:T(8,128)(2,1)S(1)} %get-tuple-element.3060) | copy-start | bytes 12292 | tf_op jit(solution)/shard_map/transpose(jvp())/while
  609.6 37.2 %copy-start.9 = (bf16[4,32,1,16,64]{4,1,3,2,0:T(8,128)(2,1)S(1)}, bf16[4,32,1,16,64]{4,1,3,2,0:T(8,128)(2,1)}, u32[]{:S(2)}) copy-start(bf16[4,32,1,16,64]{4,1,3,2,0:T(8,128)(2,1)} %get-tuple-element.1204) | copy-start | bytes 786436
  633.2 10.1 %all-to-all-start.9 = ((bf16[8,16,128]{2,1,0:T(8,128)(2,1)}), bf16[8,16,128]{2,1,0:T(8,128)(2,1)S(1)}, u32[]{:S(2)}, u32[]{:S(2)}) async-start(bf16[8,16,128]{2,1,0:T(8,128)(2,1)} %bitcast.32), calls=%async_computation.9 | async-start | bytes 65536 | tf_op jit(solution)/shard_map/all_to_all | solution.py:149
  636.5 10.8 %copy-start.6 = (bf16[16,8,1024]{2,0,1:T(8,128)(2,1)S(1)}, bf16[16,8,1024]{2,0,1:T(8,128)(2,1)}, u32[]{:S(2)}) copy-start(bf16[16,8,1024]{2,0,1:T(8,128)(2,1)} %copy-done.5) | copy-start | bytes 786436
  636.6 10.8 %copy-start.8 = (bf16[16,8,1024]{2,0,1:T(8,128)(2,1)S(1)}, bf16[16,8,1024]{2,0,1:T(8,128)(2,1)}, u32[]{:S(2)}) copy-start(bf16[16,8,1024]{2,0,1:T(8,128)(2,1)} %copy-done.7) | copy-start | bytes 786436
  638.9 20.5 %copy-start.21 = (f32[1,16]{1,0:T(1,128)S(1)}, f32[1,16]{1,0:T(1,128)}, u32[]{:S(2)}) copy-start(f32[1,16]{1,0:T(1,128)} %get-tuple-element.1210) | copy-start | bytes 196
  638.9 20.5 %copy-start.24 = (f32[1,16]{1,0:T(1,128)S(1)}, f32[1,16]{1,0:T(1,128)}, u32[]{:S(2)}) copy-start(f32[1,16]{1,0:T(1,128)} %get-tuple-element.1208) | copy-start | bytes 196
  638.9 20.5 %copy-start.27 = (f32[1,16]{1,0:T(1,128)S(1)}, f32[1,16]{1,0:T(1,128)}, u32[]{:S(2)}) copy-start(f32[1,16]{1,0:T(1,128)} %get-tuple-element.1209) | copy-start | bytes 196
  643.3 12.7 %all-to-all-start.6 = ((bf16[8,16,1024]{2,1,0:T(8,128)(2,1)}), bf16[8,16,1024]{2,1,0:T(8,128)(2,1)S(1)}, u32[]{:S(2)}, u32[]{:S(2)}) async-start(bf16[8,16,1024]{2,1,0:T(8,128)(2,1)} %convert_element_type.264), calls=%async_computation.6 | async-start | bytes 524288 | tf_op jit(solution)/shard_map/all_to_all | solution.py:134
  646.8 145.2 %copy-start.1 = (bf16[16,1024]{1,0:T(8,128)(2,1)S(1)}, bf16[16,1024]{1,0:T(8,128)(2,1)}, u32[]{:S(2)}) copy-start(bf16[16,1024]{1,0:T(8,128)(2,1)} %param.21) | copy-start | bytes 98308
  656.0 135.2 %all-to-all-start.7 = ((bf16[8,16,1024]{2,1,0:T(8,128)(2,1)}), bf16[8,16,1024]{2,1,0:T(8,128)(2,1)S(1)}, u32[]{:S(2)}, u32[]{:S(2)}) async-start(bf16[8,16,1024]{2,1,0:T(8,128)(2,1)} %bitcast.28), calls=%async_computation.7 | async-start | bytes 524288 | tf_op jit(solution)/shard_map/all_to_all | solution.py:141
  (36 other events, 223.0 us)
Sparse Core Ops, SparseCore 0:
  63.6 149.3 all-gather.4
  216.4 144.9 all-gather.6
where the time goes:
time: 810 us; the launch traced here: 799 us
  other arithmetic  208 us (26%)
  blocking collectives  196 us (24%)
  waiting for transfers between devices  188 us (23%)
  matrix products  81.9 us (10%)
  local copies, waits for them, and re-layouts  66.4 us (8%)
  starting transfers between devices  38 us (5%)
  between operations  14.6 us (2%)
    select_n x128, other arithmetic, turn(): return jax.tree.map(lambda a, b: jnp.where(reached, a, b), new, before)  151 us
    all_gather x2, waiting for transfers between devices, prefix(): everything = jax.tree.map(lambda part: lax.all_gather(part, axis), array)  138 us
    psum x1, blocking collectives, shards(): lax.psum((gradients[4].reshape(-1), gradients[5].reshape(-1), gradients[6...  129 us
    all_gather x1, blocking collectives, prefix(): everything = jax.tree.map(lambda part: lax.all_gather(part, axis), array)  44.3 us
    dynamic_update_slice x20, other arithmetic, local_slab(): final_state, results = lax.scan(advance, incoming, sections_in)  24.4 us
    dot_general x12, matrix products, block_forward(): jnp.einsum('tgn,tgjp->gjpn', b_heads, weights[..., None] * x_heads, preci...  23.7 us
    dot_general x12, matrix products, block_forward(): output = jnp.einsum('gjts,sgjp->tgjp', scores, x_heads, precision=PRECISE)  21 us
    dot_general x12, matrix products, block_forward(): jnp.einsum('tgn,gjpn->tgjp', c_heads, carry_state, precision=PRECISE)  20.8 us
  transfers between devices with their start and end apart: 11, of which 10 were waited for; matrix products, arithmetic and copies ran while one was open for 13% of the time, Pallas kernels for 0%

commit v1 on v0

v1 whole, which is shorter than its diff:
```python
import functools

import jax
import jax.numpy as jnp
from jax import lax
from jax.experimental import pallas as pl
from jax.experimental.pallas import tpu as pltpu
from jax.sharding import PartitionSpec as P

ROW = 8
TOK = 16
STATE = 128
LANES = 128
HALF = 64
EARLY = 8

F32 = jnp.float32
BF16 = jnp.bfloat16
MESH = pl.DeviceIdType.MESH


def mm(a, b, ca, cb):
    return lax.dot_general(a, b, (((ca,), (cb,)), ((), ())), preferred_element_type=F32)


def mm_exact(a, b):
    return lax.dot_general(
        a,
        b,
        (((1,), (0,)), ((), ())),
        precision=lax.Precision.HIGHEST,
        preferred_element_type=F32,
    )


def loop(low, high, body):
    def step(i, carry):
        body(i)
        return carry

    lax.fori_loop(low, high, step, 0)


def bytes_wait(ref, sem):
    pltpu.make_async_copy(ref, ref, sem).wait()


def kernel(
    sizes,
    x_ref, z_ref, og_ref, b_ref, c_ref, dt_ref, bias_ref, alog_ref, skip_ref,
    gx_ref, gz_ref, gb_ref, gc_ref, gdt_ref, sums_ref,
    sxg, rxg, sbc, rzb, rbc, sdt, rdt, ysend, yrecv, out, rout, sdbc, rdbc, sgd, rgd, szo, rzo,
    ssy, rsy, ssr, rsr,
    slope, turn, cols, ecol, wcol, eg, wx, st_s, st_a, hb, gb16, y_in, dx_in, dc_in, db_in,
    ds0, dla0, rho, kap, cterm, skipsum,
    zb_send, zb_recv, xg_send, xg_recv, bc_send, bc_recv, dt_send, dt_recv, y_send, y_recv,
    out_send, out_recv, db_send, db_recv, gd_send, gd_recv, zo_send, zo_recv,
    sy_send, sy_recv, sr_send, sr_recv,
):
    slabs, row, zs, heads = sizes
    length = zs * TOK
    per = 2 * row
    seq, z = lax.axis_index("seq"), lax.axis_index("head")
    y, r = lax.div(seq, row), lax.rem(seq, row)
    mine = pl.ds(pl.multiple_of(z * TOK, TOK), TOK)

    def at(row_to, z_to):
        return (y * row + row_to, z_to)

    def send(src, dst, send_sem, recv_sem, device):
        pltpu.make_async_remote_copy(
            src_ref=src,
            dst_ref=dst,
            send_sem=send_sem,
            recv_sem=recv_sem,
            device_id=device,
            device_id_type=MESH,
        ).start()

    barrier = pltpu.get_barrier_semaphore()

    def greet(i):
        there = at(lax.rem(r + lax.div(i, zs), row), lax.rem(z + lax.rem(i, zs), zs))
        pl.semaphore_signal(barrier, inc=1, device_id=there, device_id_type=MESH)

    def greet_slab(i):
        there = (lax.rem(y + i, slabs) * row + r, z)
        pl.semaphore_signal(barrier, inc=1, device_id=there, device_id_type=MESH)

    loop(1, row * zs, greet)
    loop(1, slabs, greet_slab)

    for k in range(zs):
        sbc[k, 0] = b_ref[:, k * STATE : (k + 1) * STATE]
        sbc[k, 1] = c_ref[:, k * STATE : (k + 1) * STATE]
        sbc[k, 2, :, 0:heads] = dt_ref[...]

    def gate(d):
        span = pl.ds(pl.multiple_of(d * LANES, LANES), LANES)
        zf, of = z_ref[:, span].astype(F32), og_ref[:, span].astype(F32)
        s = jax.nn.sigmoid(zf)
        sxg[d, 0] = x_ref[:, span]
        sxg[d, 1] = (of * (zf * s)).astype(BF16)
        slope[:, span] = of * (s * (1.0 + zf * (1.0 - s)))

    loop(0, row * zs, gate)
    pl.semaphore_wait(barrier, row * zs - 1 + slabs - 1)

    pltpu.make_async_copy(sbc.at[z], rzb.at[:, mine, :], zb_recv).start()

    def send_zb(i):
        to = lax.rem(z + i, zs)
        send(sbc.at[to], rzb.at[:, mine, :], zb_send, zb_recv, at(r, to))

    loop(1, zs, send_zb)

    pltpu.make_async_copy(sxg.at[z * row + r], rxg.at[r, :, mine, :], xg_recv.at[r]).start()

    def send_xg(i):
        r_to, z_to = lax.rem(r + lax.div(i, zs), row), lax.rem(z + lax.rem(i, zs), zs)
        send(
            sxg.at[z_to * row + r_to], rxg.at[r, :, mine, :], xg_send, xg_recv.at[r], at(r_to, z_to)
        )

    loop(1, 2 * zs, send_xg)

    bytes_wait(rzb, zb_recv)
    pltpu.make_async_copy(rzb.at[pl.ds(0, 2)], rbc.at[r], bc_recv.at[r]).start()

    def send_bc(i):
        to = lax.rem(r + i, row)
        send(rzb.at[pl.ds(0, 2)], rbc.at[r], bc_send, bc_recv.at[r], at(to, z))

    loop(1, row, send_bc)

    turn[...] = jnp.transpose(rzb[2].astype(F32)[:, 0:heads])
    raw = turn[pl.ds(pl.multiple_of(z * per, per), per), :]
    head_at = lax.broadcasted_iota(jnp.int32, (per, length), 0)
    token_at = lax.broadcasted_iota(jnp.int32, (per, length), 1)
    bias = jnp.zeros((per, length), F32)
    rate = jnp.zeros((per, length), F32)
    for h in range(per):
        bias = jnp.where(head_at == h, bias_ref[h], bias)
        rate = jnp.where(head_at == h, alog_ref[h], rate)
    pre = raw + bias
    step = jnp.maximum(pre, 0.0) + jnp.log1p(jnp.exp(-jnp.abs(pre)))
    squash = jax.nn.sigmoid(pre)
    decay = -jnp.exp(rate) * step
    cum = decay
    reach = 1
    while reach < length:
        cum = cum + jnp.where(token_at >= reach, pltpu.roll(cum, reach, 1), 0.0)
        reach *= 2
    for d in range(row):
        pair = slice(2 * d, 2 * d + 2)
        sdt[d] = jnp.concatenate([step[pair], cum[pair], squash[pair], decay[pair]], axis=0)
    pltpu.make_async_copy(sdt.at[r], rdt.at[r], dt_recv.at[r]).start()

    def send_dt(i):
        to = lax.rem(r + i, row)
        send(sdt.at[to], rdt.at[r], dt_send, dt_recv.at[r], at(to, z))

    loop(1, row, send_dt)
    loop(2 * zs, row * zs, send_xg)

    lane = lax.broadcasted_iota(jnp.int32, (1, LANES), 1)
    first = lane < HALF
    sel = [first.astype(F32), 1.0 - first.astype(F32)]
    skip = jnp.where(first, skip_ref[2 * r], skip_ref[2 * r + 1])
    at_row = lax.broadcasted_iota(jnp.int32, (length, length), 0)
    at_col = lax.broadcasted_iota(jnp.int32, (length, length), 1)
    causal = at_row >= at_col
    before = (at_row < at_col).astype(F32)
    sel_at = lax.broadcasted_iota(jnp.int32, (16, LANES), 0)
    sel_lane = lax.broadcasted_iota(jnp.int32, (16, LANES), 1)
    pick = jnp.where(sel_at == lax.div(sel_lane, HALF), 1.0, 0.0)

    def last_decay(c):
        rows = rdt[c]
        return jnp.exp(jnp.where(first, rows[2:3, length - 1 :], rows[3:4, length - 1 :]))

    def outer(c):
        rows = rdt[c]
        across = jnp.transpose(rows)
        cols[c] = across
        up = jnp.where(first, across[:, 2:3], across[:, 3:4])
        end = jnp.where(first, rows[2:3, length - 1 :], rows[3:4, length - 1 :])
        size = jnp.where(first, across[:, 0:1], across[:, 1:2])
        e = jnp.exp(up)
        w = jnp.exp(end - up) * size
        ecol[c] = e
        wcol[c] = w
        grown = (w * rxg[c, 0].astype(F32)).astype(BF16)
        faded = (e * rxg[c, 1].astype(F32)).astype(BF16)
        wx[c] = grown
        eg[c] = faded
        st_s[c] = mm(rbc[c, 0], grown, 0, 0)
        st_a[c] = mm(rbc[c, 1], faded, 0, 0)

    def inner(c):
        xs, gs, bs, cs = rxg[c, 0], rxg[c, 1], rbc[c, 0], rbc[c, 1]
        xf, gf = xs.astype(F32), gs.astype(F32)
        across = cols[c]
        aff = mm(cs, bs, 1, 1)
        y_sum = skip * xf
        dx_sum = skip * gf
        pulls = jnp.zeros((length, length), F32)
        for j in range(2):
            x_j, g_j = (xf * sel[j]).astype(BF16), (gf * sel[j]).astype(BF16)
            size = rdt[c, j : j + 1, :]
            fall = across[:, 2 + j : 3 + j] - rdt[c, 2 + j : 3 + j, :]
            e = jnp.where(causal, jnp.exp(fall), 0.0)
            dots = mm(g_j, xs, 1, 1)
            ea = e * aff
            score = (ea * size).astype(BF16)
            k0 = ea * dots
            ds0[c, j : j + 1, :] = jnp.sum(k0, axis=0, keepdims=True)
            crossing = mm((k0 * size).astype(BF16), before.astype(BF16), 1, 0)
            dla0[c, j : j + 1, :] = jnp.sum(
                jnp.where(causal, crossing, 0.0), axis=0, keepdims=True
            )
            pulls = pulls + e * dots * size
            y_sum = y_sum + mm(score, x_j, 1, 0)
            dx_sum = dx_sum + mm(score, g_j, 0, 0)
        pulls = pulls.astype(BF16)
        y_in[c] = y_sum
        dx_in[c] = dx_sum
        dc_in[c] = mm(pulls, bs, 1, 0)
        db_in[c] = mm(pulls, cs, 0, 0)
        skipsum[...] = skipsum[...] + jnp.sum(xf * gf, axis=0, keepdims=True)

    skipsum[...] = jnp.zeros_like(skipsum)

    def arrive(k):
        c = lax.rem(r + row - k, row)
        bytes_wait(rbc.at[c], bc_recv.at[c])
        bytes_wait(rdt.at[c], dt_recv.at[c])
        bytes_wait(rxg.at[c], xg_recv.at[c])
        outer(c)

        @pl.when(k < EARLY)
        def _():
            inner(c)

    loop(0, row, arrive)

    state = jnp.zeros((STATE, LANES), F32)
    back = jnp.zeros((STATE, LANES), F32)
    keep = jnp.ones((1, LANES), F32)
    for c in range(row):
        fade = last_decay(c)
        keep = keep * fade
        state = fade * state + st_s[c]
    for c in reversed(range(row)):
        back = last_decay(c) * back + st_a[c]
    high = keep.astype(BF16).astype(F32)
    mid = (keep - high).astype(BF16).astype(F32)
    low = keep - high - mid
    tail_at = lax.broadcasted_iota(jnp.int32, (16, LANES), 0)
    tail = jnp.where(tail_at == 0, high, jnp.where(tail_at == 1, mid, low)).astype(BF16)
    ysend[0, 0:STATE] = state.astype(BF16)
    ysend[1, 0:STATE] = back.astype(BF16)
    ysend[0, STATE : STATE + 16] = tail
    ysend[1, STATE : STATE + 16] = tail

    def send_state(i):
        wrapped = lax.div(y + i, slabs)
        send(
            ysend.at[wrapped],
            yrecv.at[y],
            y_send,
            y_recv.at[y],
            (lax.rem(y + i, slabs) * row + r, z),
        )

    loop(1, slabs, send_state)

    def late(k):
        inner(lax.rem(r + row - k, row))

    loop(EARLY, row, late)

    def await_state(i):
        source = lax.rem(y + i, slabs)
        bytes_wait(yrecv.at[source], y_recv.at[source])

    loop(1, slabs, await_state)

    state = jnp.zeros((STATE, LANES), F32)
    back = jnp.zeros((STATE, LANES), F32)
    for i in reversed(range(1, slabs)):
        for ahead in (False, True):
            source = lax.rem(y + i if ahead else y + slabs - i, slabs)
            counts = (y + i < slabs) if ahead else (y >= i)
            ends = yrecv[source, STATE : STATE + 16].astype(F32)
            fade = ends[0:1] + ends[1:2] + ends[2:3]
            part = yrecv[source, 0:STATE].astype(F32)
            if ahead:
                back = jnp.where(counts, fade * back + part, back)
            else:
                state = jnp.where(counts, fade * state + part, state)
    for c in range(row):
        hb[c] = state.astype(BF16)
        here = st_s[c]
        st_s[c] = state
        state = last_decay(c) * state + here
    for c in reversed(range(row)):
        gb16[c] = back.astype(BF16)
        fade = last_decay(c)
        over = fade * jnp.sum(st_s[c] * back, axis=0, keepdims=True)
        cterm[c] = jnp.broadcast_to(
            jnp.sum(pick[0:8] * over, axis=1, keepdims=True), (8, length)
        )
        back = fade * back + st_a[c]

    pick16 = pick.astype(BF16)

    def finish(k):
        c = lax.rem(r + k, row)
        xs, gs, bs, cs = rxg[c, 0], rxg[c, 1], rbc[c, 0], rbc[c, 1]
        h, g = hb[c], gb16[c]
        dc = dc_in[c] + mm(eg[c], h, 1, 1)
        db = db_in[c] + mm(wx[c], g, 1, 1)
        sdbc[c, 0] = db.astype(BF16)
        sdbc[c, 1] = dc.astype(BF16)

        @pl.when(k > 0)
        def _():
            send(sdbc.at[c], rdbc.at[r], db_send, db_recv.at[r], at(c, z))

        yi = ecol[c] * mm(cs, h, 1, 0)
        bi = wcol[c] * mm(bs, g, 1, 0)
        out[c, 0] = (dx_in[c] + bi).astype(BF16)
        out[c, 1] = (y_in[c] + yi).astype(BF16)
        there = pl.ds(pl.multiple_of((z * row + r) * LANES, LANES), LANES)

        @pl.when(k == 0)
        def _():
            pltpu.make_async_copy(sdbc.at[c], rdbc.at[r], db_recv.at[r]).start()
            pltpu.make_async_copy(out.at[c, :, mine, :], rout.at[:, :, there], out_recv).start()

        @pl.when(k > 0)
        def _():
            send(out.at[c, :, mine, :], rout.at[:, :, there], out_send, out_recv, at(c, z))

        def send_out(i):
            z_to = lax.rem(z + i, zs)
            part = pl.ds(pl.multiple_of(z_to * TOK, TOK), TOK)
            send(out.at[c, :, part, :], rout.at[:, :, there], out_send, out_recv, at(c, z_to))

        loop(1, zs, send_out)
        rho[c] = mm(pick16, (gs.astype(F32) * yi).astype(BF16), 1, 1)[0:8]
        kap[c] = mm(pick16, (xs.astype(F32) * bi).astype(BF16), 1, 1)[0:8]

    loop(0, row, finish)

    flat = (row * 8, length)
    dla = (
        dla0[...].reshape(flat)
        + mm_exact(rho[...].reshape(flat), causal.astype(F32))
        + mm_exact(kap[...].reshape(flat), before)
        + cterm[...].reshape(flat)
    )
    parts = [rdt[c] for c in range(row)]
    steps = jnp.concatenate(parts, axis=0)
    squashes = jnp.concatenate([pltpu.roll(p, 4, 0) for p in parts], axis=0)
    decays = jnp.concatenate([pltpu.roll(p, 2, 0) for p in parts], axis=0)
    which = lax.rem(lax.broadcasted_iota(jnp.int32, flat, 0), 8)
    rates = jnp.exp(jnp.where(which == 0, alog_ref[2 * r], alog_ref[2 * r + 1]))
    dsteps = ds0[...].reshape(flat) + kap[...].reshape(flat) / steps - rates * dla
    draws = jnp.where(which < 2, dsteps * squashes, 0.0)
    dlogs = jnp.where(which < 2, dla * decays, 0.0)
    sgd[...] = draws.reshape(row, 8, length)
    pltpu.make_async_copy(sgd.at[r], rgd.at[r], gd_recv.at[r]).start()

    def send_gd(i):
        to = lax.rem(r + i, row)
        send(sgd.at[to], rgd.at[r], gd_send, gd_recv.at[r], at(to, z))

    loop(1, row, send_gd)

    sum_at = lax.broadcasted_iota(jnp.int32, (8, LANES), 0)
    sum_lane = lax.broadcasted_iota(jnp.int32, (8, LANES), 1)
    sums = jnp.zeros((8, LANES), F32)
    for j in range(2):
        totals = (
            jnp.sum(jnp.where(which == j, draws, 0.0)),
            jnp.sum(jnp.where(which == j, dlogs, 0.0)),
            jnp.sum(skipsum[...] * sel[j]),
        )
        for q in range(3):
            place = (sum_at == q) & (sum_lane == 2 * r + j)
            sums = jnp.where(place, totals[q], sums)
    ssy[...] = sums
    pltpu.make_async_copy(ssy, rsy.at[y], sy_recv).start()

    def send_sy(i):
        send(ssy, rsy.at[y], sy_send, sy_recv, (lax.rem(y + i, slabs) * row + r, z))

    loop(1, slabs, send_sy)

    loop(0, row, lambda c: bytes_wait(rdbc.at[c], db_recv.at[c]))
    for q in range(2):
        total = rdbc[0, q].astype(F32)
        for c in range(1, row):
            total = total + rdbc[c, q].astype(F32)
        szo[q] = total.astype(BF16)
    loop(0, row, lambda c: bytes_wait(rgd.at[c], gd_recv.at[c]))
    turn[...] = jnp.zeros_like(turn)
    turn[pl.ds(pl.multiple_of(z * per, per), per), :] = jnp.concatenate(
        [rgd[c][0:2] for c in range(row)], axis=0
    )
    szo[2, :, 0:heads] = jnp.transpose(turn[...]).astype(BF16)
    pltpu.make_async_copy(szo.at[:, mine, :], rzo.at[z], zo_recv).start()

    def send_zo(i):
        to = lax.rem(z + i, zs)
        part = pl.ds(pl.multiple_of(to * TOK, TOK), TOK)
        send(szo.at[:, part, :], rzo.at[z], zo_send, zo_recv, at(r, to))

    loop(1, zs, send_zo)

    bytes_wait(rsy, sy_recv)
    total = rsy[0]
    for i in range(1, slabs):
        total = total + rsy[i]
    ssr[...] = total
    pltpu.make_async_copy(ssr, rsr.at[r], sr_recv).start()

    def send_sr(i):
        send(ssr, rsr.at[r], sr_send, sr_recv, at(lax.rem(r + i, row), z))

    loop(1, row, send_sr)

    bytes_wait(rout, out_recv)
    gx_ref[...] = rout[0]

    def gate_back(d):
        span = pl.ds(pl.multiple_of(d * LANES, LANES), LANES)
        gz_ref[:, span] = (slope[:, span] * rout[1, :, span].astype(F32)).astype(BF16)

    loop(0, row * zs, gate_back)

    bytes_wait(rzo, zo_recv)
    total = jnp.zeros((TOK, heads), F32)
    for k in range(zs):
        gb_ref[:, k * STATE : (k + 1) * STATE] = rzo[k, 0]
        gc_ref[:, k * STATE : (k + 1) * STATE] = rzo[k, 1]
        total = total + rzo[k, 2, :, 0:heads].astype(F32)
    gdt_ref[...] = total.astype(BF16)
    bytes_wait(rsr, sr_recv)
    total = rsr[0]
    for i in range(1, row):
        total = total + rsr[i]
    sums_ref[...] = total

    bytes_wait(sbc.at[pl.ds(0, zs - 1)], zb_send)
    bytes_wait(sxg.at[pl.ds(0, row * zs - 1)], xg_send)
    bytes_wait(rbc.at[pl.ds(0, row - 1)], bc_send)
    bytes_wait(sdt.at[pl.ds(0, row - 1)], dt_send)
    bytes_wait(yrecv.at[pl.ds(0, slabs - 1)], y_send)
    bytes_wait(sxg.at[pl.ds(0, row * zs - 1)], out_send)
    bytes_wait(rdbc.at[pl.ds(0, row - 1)], db_send)
    bytes_wait(sgd.at[pl.ds(0, row - 1)], gd_send)
    bytes_wait(rzo.at[pl.ds(0, zs - 1)], zo_send)
    bytes_wait(rsy.at[pl.ds(0, slabs - 1)], sy_send)
    bytes_wait(rsr.at[pl.ds(0, row - 1)], sr_send)


def shards(row, x_proj, z_gate, out_grad, b_proj, c_proj, dt_raw, dt_bias, a_log, d_skip):
    zs = lax.axis_size("head")
    slabs = lax.axis_size("seq") // row
    heads = 2 * row * zs
    length = zs * TOK
    inner = heads * HALF

    def vmem(*shape, dtype=BF16):
        return pltpu.VMEM(shape, dtype)

    square = (row, length, LANES)
    states = (row, STATE, LANES)
    scratch = [
        vmem(row * zs, 2, TOK, LANES),
        vmem(row, 2, length, LANES),
        vmem(zs, 3, TOK, STATE),
        vmem(3, length, STATE),
        vmem(row, 2, length, STATE),
        vmem(row, 8, length, dtype=F32),
        vmem(row, 8, length, dtype=F32),
        vmem(2, STATE + 16, LANES),
        vmem(slabs, STATE + 16, LANES),
        vmem(row, 2, length, LANES),
        vmem(2, TOK, inner),
        vmem(row, 2, length, STATE),
        vmem(row, 2, length, STATE),
        vmem(row, 8, length, dtype=F32),
        vmem(row, 8, length, dtype=F32),
        vmem(3, length, STATE),
        vmem(zs, 3, TOK, STATE),
        vmem(8, LANES, dtype=F32),
        vmem(slabs, 8, LANES, dtype=F32),
        vmem(8, LANES, dtype=F32),
        vmem(row, 8, LANES, dtype=F32),
        vmem(TOK, inner, dtype=F32),
        vmem(heads, length, dtype=F32),
        vmem(row, length, 8, dtype=F32),
        vmem(*square, dtype=F32),
        vmem(*square, dtype=F32),
        vmem(*square),
        vmem(*square),
        vmem(*states, dtype=F32),
        vmem(*states, dtype=F32),
        vmem(*states),
        vmem(*states),
        vmem(*square, dtype=F32),
        vmem(*square, dtype=F32),
        vmem(*square, dtype=F32),
        vmem(*square, dtype=F32),
        vmem(row, 8, length, dtype=F32),
        vmem(row, 8, length, dtype=F32),
        vmem(row, 8, length, dtype=F32),
        vmem(row, 8, length, dtype=F32),
        vmem(row, 8, length, dtype=F32),
        vmem(1, LANES, dtype=F32),
    ]
    one, many = pltpu.SemaphoreType.DMA, lambda n: pltpu.SemaphoreType.DMA((n,))
    semaphores = [
        one, one,
        one, many(row),
        one, many(row),
        one, many(row),
        one, many(slabs),
        one, one,
        one, many(row),
        one, many(row),
        one, one,
        one, one,
        one, one,
    ]
    in_vmem = pl.BlockSpec(memory_space=pltpu.VMEM)
    in_smem = pl.BlockSpec(memory_space=pltpu.SMEM)
    like = jax.ShapeDtypeStruct
    results = pl.pallas_call(
        functools.partial(kernel, (slabs, row, zs, heads)),
        out_shape=[
            like((TOK, inner), BF16),
            like((TOK, inner), BF16),
            like((TOK, zs * STATE), BF16),
            like((TOK, zs * STATE), BF16),
            like((TOK, heads), BF16),
            like((8, LANES), F32),
        ],
        in_specs=[in_vmem] * 6 + [in_smem] * 3,
        out_specs=[in_vmem] * 6,
        scratch_shapes=scratch + semaphores,
        compiler_params=pltpu.CompilerParams(
            collective_id=0, has_side_effects=True, vmem_limit_bytes=40 * 2**20
        ),
        name="scan_backward",
    )(x_proj, z_gate, out_grad, b_proj, c_proj, dt_raw, dt_bias, a_log, d_skip)
    per = 2 * row
    sums = results[5]
    return (*results[:5], sums[0, :per], sums[1, :per], sums[2, :per])


def solution(mesh, row=ROW):
    tokens = P(("seq", "head"), None)
    return jax.shard_map(
        functools.partial(shards, row),
        mesh=mesh,
        in_specs=(tokens,) * 6 + (P("head"),) * 3,
        out_specs=(tokens,) * 5 + (P("head"),) * 3,
        check_vma=False,
    )
```

time: 810 us -> 82.8 us (0.10); the launches traced: 799 us -> 82.4 us
  other arithmetic: 208 us -> 0 us
  blocking collectives: 196 us -> 0 us
  waiting for transfers between devices: 188 us -> 0 us
  matrix products: 81.9 us -> 0 us
  Pallas kernels: 0 us -> 71 us
  local copies, waits for them, and re-layouts: 66.4 us -> 10.8 us
  starting transfers between devices: 38 us -> 0 us
  between operations: 14.6 us -> 0.67 us
    select_n x128 -> x0, other arithmetic: 151 us -> none  [turn(): return jax.tree.map(lambda a, b: jnp.where(reached, a, b), new, before)]
    all_gather x2 -> x0, waiting for transfers between devices: 138 us -> none  [prefix(): everything = jax.tree.map(lambda part: lax.all_gather(part, axis), array)]
    psum x1 -> x0, blocking collectives: 129 us -> none  [shards(): lax.psum((gradients[4].reshape(-1), gradients[5].reshape(-1), gradients[6...]
    dot_general x50 -> x0, matrix products: 81.9 us -> none  [the longest x12 23.7 us: block_forward(): jnp.einsum('tgn,tgjp->gjpn', b_heads, weights[..., None] * x_heads, preci...]
    pallas_call x0 -> x1, Pallas kernels: none -> 71 us  [shards(): pl.pallas_call(functools.partial(kernel, (slabs, row, zs, heads)), out_sh...]
    all_to_all x9 -> x0, waiting for transfers between devices: 50 us -> none  [the longest x1 7.96 us: shards(): lax.all_to_all(x_proj, 'head', split_axis=1, concat_axis=0, tiled=True)]
    all_gather x1 -> x0, blocking collectives: 44.3 us -> none  [prefix(): everything = jax.tree.map(lambda part: lax.all_gather(part, axis), array)]
    all_to_all x9 -> x0, starting transfers between devices: 38 us -> none  [the longest x1 10.9 us: shards(): lax.all_to_all(dt_raw, 'head', split_axis=1, concat_axis=0, tiled=True)]
  transfers between devices with their start and end apart: 11 -> 0, of which waited for: 10 -> 0; matrix products, arithmetic and copies ran while one was open for 13% -> 0% of each run, Pallas kernels for 0% -> 0%
where the time goes in v1:
time: 82.8 us; the launch traced here: 82.4 us
  Pallas kernels  71 us (86%)
  local copies, waits for them, and re-layouts  10.8 us (13%)
    pallas_call x1, Pallas kernels, shards(): pl.pallas_call(functools.partial(kernel, (slabs, row, zs, heads)), out_sh...  71 us
    unnamed x23, local copies, waits for them, and re-layouts  10.2 us

profile of v1, /device:TPU:1, one launch (start us, length us, event | category | flops | bytes accessed | tf_op | source)
XLA Modules:
  0.0 82.4 jit_solution(7486714434241021048)
XLA Ops:
  0.6 0.0 copy-start
  0.6 0.9 %copy-done = bf16[16,8192]{1,0:T(8,128)(2,1)S(1)} copy-done((bf16[16,8192]{1,0:T(8,128)(2,1)S(1)}, bf16[16,8192]{1,0:T(8,128)(2,1)}, u32[]{:S(2)}) %copy-start) | copy-done | bytes 262168
  1.6 0.0 copy-start.1
  1.6 0.9 %copy-done.1 = bf16[16,8192]{1,0:T(8,128)(2,1)S(1)} copy-done((bf16[16,8192]{1,0:T(8,128)(2,1)S(1)}, bf16[16,8192]{1,0:T(8,128)(2,1)}, u32[]{:S(2)}) %copy-start.1) | copy-done | bytes 262168
  2.5 0.0 copy-start.2
  2.5 0.9 %copy-done.2 = bf16[16,8192]{1,0:T(8,128)(2,1)S(1)} copy-done((bf16[16,8192]{1,0:T(8,128)(2,1)S(1)}, bf16[16,8192]{1,0:T(8,128)(2,1)}, u32[]{:S(2)}) %copy-start.2) | copy-done | bytes 262168
  3.5 0.0 copy-start.3
  3.5 0.8 copy-done.3
  4.2 0.0 copy-start.4
  4.3 0.8 copy-done.4
  5.0 0.0 copy-start.5
  5.0 0.7 copy-done.5
  5.7 0.0 copy-start.6
  5.7 0.7 copy-done.6
  6.4 0.0 copy-start.7
  6.4 0.7 copy-done.7
  7.0 0.0 copy-start.8
  7.0 0.7 copy-done.8
  7.7 71.0 %scan_backward.1 = (bf16[16,8192]{1,0:T(8,128)(2,1)S(1)}, bf16[16,8192]{1,0:T(8,128)(2,1)S(1)}, bf16[16,1024]{1,0:T(8,128)(2,1)S(1)}, bf16[16,1024]{1,0:T(8,128)...) custom-call(bf16[16,8192]{1,0:T(8,128)(2,1)S(1)} %copy-done, bf16[16,8192]{1,0:T(8,128)(2,1)S(1)} %copy-done.1, ...), custom_call_target="tpu_custom_call" | custom-call | tf_op jit(solution)/shard_map/scan_backward/pallas_call | solution.py:543
  78.7 0.5 slice_bitcast_fusion
  79.2 0.7 copy.22
  79.9 0.7 copy.23
  80.6 0.6 copy.24
  81.2 0.6 copy.25
  81.8 0.6 copy.26
Async XLA Ops:
  0.6 1.0 %copy-start = (bf16[16,8192]{1,0:T(8,128)(2,1)S(1)}, bf16[16,8192]{1,0:T(8,128)(2,1)}, u32[]{:S(2)}) copy-start(bf16[16,8192]{1,0:T(8,128)(2,1)} %x_ref.1) | copy-start | bytes 786436
  1.6 0.9 %copy-start.1 = (bf16[16,8192]{1,0:T(8,128)(2,1)S(1)}, bf16[16,8192]{1,0:T(8,128)(2,1)}, u32[]{:S(2)}) copy-start(bf16[16,8192]{1,0:T(8,128)(2,1)} %z_ref.1) | copy-start | bytes 786436
  2.5 0.9 %copy-start.2 = (bf16[16,8192]{1,0:T(8,128)(2,1)S(1)}, bf16[16,8192]{1,0:T(8,128)(2,1)}, u32[]{:S(2)}) copy-start(bf16[16,8192]{1,0:T(8,128)(2,1)} %og_ref.1) | copy-start | bytes 786436
  3.5 0.8 copy-start.3
  4.2 0.8 copy-start.4
  5.0 0.7 copy-start.5
  5.7 0.7 copy-start.6
  6.4 0.7 copy-start.7
  7.0 0.7 copy-start.8

commit v2 on v1

v2 whole, which is shorter than its diff:
```python
import functools

import jax
import jax.numpy as jnp
from jax import lax
from jax.experimental import pallas as pl
from jax.experimental.pallas import tpu as pltpu
from jax.sharding import PartitionSpec as P

ROW = 8
TOK = 16
STATE = 128
LANES = 128
HALF = 64
AHEAD = 4

F32 = jnp.float32
BF16 = jnp.bfloat16
MESH = pl.DeviceIdType.MESH


def mm(a, b, ca, cb):
    return lax.dot_general(a, b, (((ca,), (cb,)), ((), ())), preferred_element_type=F32)


def mm_exact(a, b):
    return lax.dot_general(
        a,
        b,
        (((1,), (0,)), ((), ())),
        precision=lax.Precision.HIGHEST,
        preferred_element_type=F32,
    )


def loop(low, high, body):
    def step(i, carry):
        body(i)
        return carry

    lax.fori_loop(low, high, step, 0)


def bytes_wait(ref, sem):
    pltpu.make_async_copy(ref, ref, sem).wait()


def kernel(
    sizes,
    x_hbm, z_hbm, og_hbm, b_hbm, c_hbm, dt_hbm, bias_hbm, alog_hbm, skip_hbm,
    inner_ref, outer_ref, gdt_ref, sums_ref,
    x_ref, z_ref, og_ref, b_ref, c_ref, dt_ref, bias_ref, alog_ref, skip_ref,
    sg, rx, rg, sbc, rzb, rb, rc, sdt, rdt, ssend, asend, srecv, arecv, sy, sdx, ry, rdx,
    sdb, sdc, rdb, rdc, sgd, rgd, szo, rzo, ssy, rsy, ssr, rsr,
    slope, turn, cols, ecol, wcol, eg, wx, st_s, st_a, hb, affs, decs, scores,
    y_in, dx_in, db_in, ds0, dla0, rho, kap, cterm, skipsum,
    zb_send, zb_recv, x_send, x_recv, g_send, g_recv, b_send, b_recv, c_send, c_recv,
    dt_send, dt_recv, s_send, s_recv, a_send, a_recv, y_send, y_recv, dx_send, dx_recv,
    db_send, db_recv, dc_send, dc_recv, gd_send, gd_recv, zo_send, zo_recv,
    sy_send, sy_recv, sr_send, sr_recv, load,
):
    slabs, row, zs, heads = sizes
    length = zs * TOK
    per = 2 * row
    seq, z = lax.axis_index("seq"), lax.axis_index("head")
    y, r = lax.div(seq, row), lax.rem(seq, row)
    mine = pl.ds(pl.multiple_of(z * TOK, TOK), TOK)

    def at(row_to, z_to):
        return (y * row + row_to, z_to)

    def other(i):
        return lax.rem(r + lax.div(i, zs), row), lax.rem(z + lax.rem(i, zs), zs)

    def lanes_of(d):
        return pl.ds(pl.multiple_of(d * LANES, LANES), LANES)

    def tokens_of(k):
        return pl.ds(pl.multiple_of(k * TOK, TOK), TOK)

    def send(src, dst, send_sem, recv_sem, device):
        pltpu.make_async_remote_copy(
            src_ref=src,
            dst_ref=dst,
            send_sem=send_sem,
            recv_sem=recv_sem,
            device_id=device,
            device_id_type=MESH,
        ).start()

    def keep(src, dst, recv_sem):
        pltpu.make_async_copy(src, dst, recv_sem).start()

    loads = [
        pltpu.make_async_copy(there, here, load.at[i])
        for i, (there, here) in enumerate(
            (
                (b_hbm, b_ref),
                (c_hbm, c_ref),
                (dt_hbm, dt_ref),
                (x_hbm, x_ref),
                (z_hbm, z_ref),
                (og_hbm, og_ref),
                (bias_hbm, bias_ref),
                (alog_hbm, alog_ref),
                (skip_hbm, skip_ref),
            )
        )
    ]
    for copy in loads:
        copy.start()

    barrier = pltpu.get_barrier_semaphore()

    def greet(i):
        pl.semaphore_signal(barrier, inc=1, device_id=at(*other(i)), device_id_type=MESH)

    def greet_slab(i):
        there = (lax.rem(y + i, slabs) * row + r, z)
        pl.semaphore_signal(barrier, inc=1, device_id=there, device_id_type=MESH)

    loop(1, row * zs, greet)
    loop(1, slabs, greet_slab)

    for copy in loads[:3]:
        copy.wait()
    for k in range(zs):
        sbc[k, 0] = b_ref[:, k * STATE : (k + 1) * STATE]
        sbc[k, 1] = c_ref[:, k * STATE : (k + 1) * STATE]
        sbc[k, 2, :, 0:heads] = dt_ref[...]
    loads[3].wait()
    pl.semaphore_wait(barrier, row * zs - 1 + slabs - 1)

    keep(sbc.at[z], rzb.at[:, mine, :], zb_recv)

    def send_zb(i):
        to = lax.rem(z + i, zs)
        send(sbc.at[to], rzb.at[:, mine, :], zb_send, zb_recv, at(r, to))

    loop(1, zs, send_zb)

    keep(x_ref.at[:, lanes_of(z * row + r)], rx.at[r, mine, :], x_recv.at[r])

    def send_x(i):
        r_to, z_to = other(i)
        send(
            x_ref.at[:, lanes_of(z_to * row + r_to)],
            rx.at[r, mine, :],
            x_send,
            x_recv.at[r],
            at(r_to, z_to),
        )

    loop(1, AHEAD * zs, send_x)

    bytes_wait(rzb, zb_recv)
    keep(rzb.at[0], rb.at[r], b_recv.at[r])
    keep(rzb.at[1], rc.at[r], c_recv.at[r])

    def send_b(i):
        to = lax.rem(r + i, row)
        send(rzb.at[0], rb.at[r], b_send, b_recv.at[r], at(to, z))

    loop(1, row, send_b)

    for copy in loads[4:]:
        copy.wait()
    turn[...] = jnp.transpose(rzb[2].astype(F32)[:, 0:heads])
    raw = turn[pl.ds(pl.multiple_of(z * per, per), per), :]
    head_at = lax.broadcasted_iota(jnp.int32, (per, length), 0)
    token_at = lax.broadcasted_iota(jnp.int32, (per, length), 1)
    bias = jnp.zeros((per, length), F32)
    rate = jnp.zeros((per, length), F32)
    for h in range(per):
        bias = jnp.where(head_at == h, bias_ref[h], bias)
        rate = jnp.where(head_at == h, alog_ref[h], rate)
    pre = raw + bias
    step = jnp.maximum(pre, 0.0) + jnp.log1p(jnp.exp(-jnp.abs(pre)))
    squash = jax.nn.sigmoid(pre)
    decay = -jnp.exp(rate) * step
    cum = decay
    reach = 1
    while reach < length:
        cum = cum + jnp.where(token_at >= reach, pltpu.roll(cum, reach, 1), 0.0)
        reach *= 2
    for d in range(row):
        pair = slice(2 * d, 2 * d + 2)
        sdt[d] = jnp.concatenate([step[pair], cum[pair], squash[pair], decay[pair]], axis=0)
    keep(sdt.at[r], rdt.at[r], dt_recv.at[r])

    def send_dt(i):
        to = lax.rem(r + i, row)
        send(sdt.at[to], rdt.at[r], dt_send, dt_recv.at[r], at(to, z))

    loop(1, row, send_dt)
    loop(AHEAD * zs, row * zs, send_x)

    def send_c(i):
        to = lax.rem(r + i, row)
        send(rzb.at[1], rc.at[r], c_send, c_recv.at[r], at(to, z))

    loop(1, row, send_c)

    def gate(d):
        zf, of = z_ref[:, lanes_of(d)].astype(F32), og_ref[:, lanes_of(d)].astype(F32)
        s = jax.nn.sigmoid(zf)
        sg[d] = (of * (zf * s)).astype(BF16)
        slope[:, lanes_of(d)] = of * (s * (1.0 + zf * (1.0 - s)))

    gate(z * row + r)
    keep(sg.at[z * row + r], rg.at[r, mine, :], g_recv.at[r])

    def send_g(i):
        r_to, z_to = other(i)
        d = z_to * row + r_to
        gate(d)
        send(sg.at[d], rg.at[r, mine, :], g_send, g_recv.at[r], at(r_to, z_to))

    loop(1, row * zs, send_g)

    lane = lax.broadcasted_iota(jnp.int32, (1, LANES), 1)
    first = lane < HALF
    sel = [first.astype(F32), 1.0 - first.astype(F32)]
    skip = jnp.where(first, skip_ref[2 * r], skip_ref[2 * r + 1])
    at_row = lax.broadcasted_iota(jnp.int32, (length, length), 0)
    at_col = lax.broadcasted_iota(jnp.int32, (length, length), 1)
    causal = at_row >= at_col
    before = (at_row < at_col).astype(F32)
    sel_at = lax.broadcasted_iota(jnp.int32, (16, LANES), 0)
    sel_lane = lax.broadcasted_iota(jnp.int32, (16, LANES), 1)
    pick = jnp.where(sel_at == lax.div(sel_lane, HALF), 1.0, 0.0)
    pick16 = pick.astype(BF16)

    def chunk(k):
        return lax.rem(r + row - k, row)

    def last_decay(c):
        rows = rdt[c]
        return jnp.exp(jnp.where(first, rows[2:3, length - 1 :], rows[3:4, length - 1 :]))

    def with_keep(total, keep_all):
        high = keep_all.astype(BF16).astype(F32)
        mid = (keep_all - high).astype(BF16).astype(F32)
        low = keep_all - high - mid
        tail = jnp.where(sel_at == 0, high, jnp.where(sel_at == 1, mid, low))
        return jnp.concatenate([total.astype(BF16), tail.astype(BF16)], axis=0)

    def states(k):
        c = chunk(k)
        bytes_wait(rdt.at[c], dt_recv.at[c])
        rows = rdt[c]
        across = jnp.transpose(rows)
        cols[c] = across
        up = jnp.where(first, across[:, 2:3], across[:, 3:4])
        end = jnp.where(first, rows[2:3, length - 1 :], rows[3:4, length - 1 :])
        size = jnp.where(first, across[:, 0:1], across[:, 1:2])
        w = jnp.exp(end - up) * size
        ecol[c] = jnp.exp(up)
        wcol[c] = w
        bytes_wait(rb.at[c], b_recv.at[c])
        bytes_wait(rx.at[c], x_recv.at[c])
        grown = (w * rx[c].astype(F32)).astype(BF16)
        wx[c] = grown
        st_s[c] = mm(rb[c], grown, 0, 0)

    loop(0, row, states)
    state = jnp.zeros((STATE, LANES), F32)
    keep_all = jnp.ones((1, LANES), F32)
    for c in range(row):
        fade = last_decay(c)
        keep_all = keep_all * fade
        state = fade * state + st_s[c]
    ssend[...] = with_keep(state, keep_all)

    def send_s(i):
        @pl.when(y + i < slabs)
        def _():
            send(ssend, srecv.at[y], s_send, s_recv.at[y], ((y + i) * row + r, z))

    loop(1, slabs, send_s)

    def scored(k):
        c = chunk(k)
        bytes_wait(rc.at[c], c_recv.at[c])
        xf = rx[c].astype(F32)
        across = cols[c]
        aff = mm(rc[c], rb[c], 1, 1)
        affs[c] = aff
        y_sum = skip * xf
        for j in range(2):
            fall = across[:, 2 + j : 3 + j] - rdt[c, 2 + j : 3 + j, :]
            e = jnp.where(causal, jnp.exp(fall), 0.0)
            decs[c, j] = e
            score = (e * aff * rdt[c, j : j + 1, :]).astype(BF16)
            scores[c, j] = score
            y_sum = y_sum + mm(score, (xf * sel[j]).astype(BF16), 1, 0)
        y_in[c] = y_sum

    loop(0, row, scored)

    def cotangents(k):
        c = chunk(k)
        bytes_wait(rg.at[c], g_recv.at[c])
        faded = (ecol[c] * rg[c].astype(F32)).astype(BF16)
        eg[c] = faded
        st_a[c] = mm(rc[c], faded, 0, 0)

    loop(0, row, cotangents)
    back = jnp.zeros((STATE, LANES), F32)
    for c in reversed(range(row)):
        back = last_decay(c) * back + st_a[c]
    asend[...] = with_keep(back, keep_all)

    def send_a(i):
        @pl.when(y >= i)
        def _():
            send(asend, arecv.at[y], a_send, a_recv.at[y], ((y - i) * row + r, z))

    loop(1, slabs, send_a)

    state = jnp.zeros((STATE, LANES), F32)
    srecv[y] = ssend[...]
    for i in reversed(range(1, slabs)):
        source = lax.rem(y + slabs - i, slabs)

        @pl.when(y >= i)
        def _():
            bytes_wait(srecv.at[source], s_recv.at[source])

        ends = srecv[source, STATE : STATE + 16].astype(F32)
        fade = ends[0:1] + ends[1:2] + ends[2:3]
        state = jnp.where(y >= i, fade * state + srecv[source, 0:STATE].astype(F32), state)
    for c in range(row):
        hb[c] = state.astype(BF16)
        here = st_s[c]
        st_s[c] = state
        state = last_decay(c) * state + here

    there = lanes_of(z * row + r)

    def leave(buffer, k, c, landing, send_sem, recv_sem):
        @pl.when(k == 0)
        def _():
            keep(buffer.at[c, mine, :], landing.at[:, there], recv_sem)

        @pl.when(k > 0)
        def _():
            send(buffer.at[c, mine, :], landing.at[:, there], send_sem, recv_sem, at(c, z))

        def one(i):
            to = lax.rem(z + i, zs)
            part = buffer.at[c, tokens_of(to), :]
            send(part, landing.at[:, there], send_sem, recv_sem, at(c, to))

        loop(1, zs, one)

    def finish_y(k):
        c = lax.rem(r + k, row)
        yi = ecol[c] * mm(rc[c], hb[c], 1, 0)
        sy[c] = (y_in[c] + yi).astype(BF16)
        leave(sy, k, c, ry, y_send, y_recv)
        rho[c] = mm(pick16, (rg[c].astype(F32) * yi).astype(BF16), 1, 1)[0:8]

    loop(0, row, finish_y)

    skipsum[...] = jnp.zeros_like(skipsum)

    def pulled(k):
        c = lax.rem(r + k, row)
        xs, gs, bs, cs = rx[c], rg[c], rb[c], rc[c]
        xf, gf = xs.astype(F32), gs.astype(F32)
        aff = affs[c]
        dx_sum = skip * gf
        pulls = jnp.zeros((length, length), F32)
        for j in range(2):
            g_j = (gf * sel[j]).astype(BF16)
            size = rdt[c, j : j + 1, :]
            k1 = decs[c, j] * mm(g_j, xs, 1, 1)
            k0 = k1 * aff
            ds0[c, j : j + 1, :] = jnp.sum(k0, axis=0, keepdims=True)
            crossing = mm((k0 * size).astype(BF16), before.astype(BF16), 1, 0)
            dla0[c, j : j + 1, :] = jnp.sum(
                jnp.where(causal, crossing, 0.0), axis=0, keepdims=True
            )
            pulls = pulls + k1 * size
            dx_sum = dx_sum + mm(scores[c, j], g_j, 0, 0)
        pulls = pulls.astype(BF16)
        dx_in[c] = dx_sum
        sdc[c] = (mm(pulls, bs, 1, 0) + mm(eg[c], hb[c], 1, 1)).astype(BF16)
        db_in[c] = mm(pulls, cs, 0, 0)
        skipsum[...] = skipsum[...] + jnp.sum(xf * gf, axis=0, keepdims=True)

        @pl.when(k == 0)
        def _():
            keep(sdc.at[c], rdc.at[r], dc_recv.at[r])

        @pl.when(k > 0)
        def _():
            send(sdc.at[c], rdc.at[r], dc_send, dc_recv.at[r], at(c, z))

    loop(0, row, pulled)

    back = jnp.zeros((STATE, LANES), F32)
    arecv[y] = asend[...]
    for i in reversed(range(1, slabs)):
        source = lax.rem(y + i, slabs)

        @pl.when(y + i < slabs)
        def _():
            bytes_wait(arecv.at[source], a_recv.at[source])

        ends = arecv[source, STATE : STATE + 16].astype(F32)
        fade = ends[0:1] + ends[1:2] + ends[2:3]
        part = arecv[source, 0:STATE].astype(F32)
        back = jnp.where(y + i < slabs, fade * back + part, back)
    for c in reversed(range(row)):
        hb[c] = back.astype(BF16)
        fade = last_decay(c)
        over = fade * jnp.sum(st_s[c] * back, axis=0, keepdims=True)
        cterm[c] = jnp.broadcast_to(
            jnp.sum(pick[0:8] * over, axis=1, keepdims=True), (8, length)
        )
        back = fade * back + st_a[c]

    def finish_x(k):
        c = lax.rem(r + k, row)
        bi = wcol[c] * mm(rb[c], hb[c], 1, 0)
        sdx[c] = (dx_in[c] + bi).astype(BF16)
        leave(sdx, k, c, rdx, dx_send, dx_recv)
        sdb[c] = (db_in[c] + mm(wx[c], hb[c], 1, 1)).astype(BF16)

        @pl.when(k == 0)
        def _():
            keep(sdb.at[c], rdb.at[r], db_recv.at[r])

        @pl.when(k > 0)
        def _():
            send(sdb.at[c], rdb.at[r], db_send, db_recv.at[r], at(c, z))

        kap[c] = mm(pick16, (rx[c].astype(F32) * bi).astype(BF16), 1, 1)[0:8]

    loop(0, row, finish_x)

    flat = (row * 8, length)
    dla = (
        dla0[...].reshape(flat)
        + mm_exact(rho[...].reshape(flat), causal.astype(F32))
        + mm_exact(kap[...].reshape(flat), before)
        + cterm[...].reshape(flat)
    )
    parts = [rdt[c] for c in range(row)]
    steps = jnp.concatenate(parts, axis=0)
    squashes = jnp.concatenate([pltpu.roll(p, 4, 0) for p in parts], axis=0)
    decays = jnp.concatenate([pltpu.roll(p, 2, 0) for p in parts], axis=0)
    which = lax.rem(lax.broadcasted_iota(jnp.int32, flat, 0), 8)
    rates = jnp.exp(jnp.where(which == 0, alog_ref[2 * r], alog_ref[2 * r + 1]))
    dsteps = ds0[...].reshape(flat) + kap[...].reshape(flat) / steps - rates * dla
    draws = jnp.where(which < 2, dsteps * squashes, 0.0)
    dlogs = jnp.where(which < 2, dla * decays, 0.0)
    sgd[...] = draws.reshape(row, 8, length)
    keep(sgd.at[r], rgd.at[r], gd_recv.at[r])

    def send_gd(i):
        to = lax.rem(r + i, row)
        send(sgd.at[to], rgd.at[r], gd_send, gd_recv.at[r], at(to, z))

    loop(1, row, send_gd)

    sum_at = lax.broadcasted_iota(jnp.int32, (8, LANES), 0)
    sum_lane = lax.broadcasted_iota(jnp.int32, (8, LANES), 1)
    sums = jnp.zeros((8, LANES), F32)
    for j in range(2):
        totals = (
            jnp.sum(jnp.where(which == j, draws, 0.0)),
            jnp.sum(jnp.where(which == j, dlogs, 0.0)),
            jnp.sum(skipsum[...] * sel[j]),
        )
        for q in range(3):
            place = (sum_at == q) & (sum_lane == 2 * r + j)
            sums = jnp.where(place, totals[q], sums)
    ssy[...] = sums
    keep(ssy, rsy.at[y], sy_recv)

    def send_sy(i):
        send(ssy, rsy.at[y], sy_send, sy_recv, (lax.rem(y + i, slabs) * row + r, z))

    loop(1, slabs, send_sy)

    loop(0, row, lambda c: bytes_wait(rdc.at[c], dc_recv.at[c]))
    total = rdc[0].astype(F32)
    for c in range(1, row):
        total = total + rdc[c].astype(F32)
    szo[1] = total.astype(BF16)
    loop(0, row, lambda c: bytes_wait(rdb.at[c], db_recv.at[c]))
    total = rdb[0].astype(F32)
    for c in range(1, row):
        total = total + rdb[c].astype(F32)
    szo[0] = total.astype(BF16)
    loop(0, row, lambda c: bytes_wait(rgd.at[c], gd_recv.at[c]))
    turn[...] = jnp.zeros_like(turn)
    turn[pl.ds(pl.multiple_of(z * per, per), per), :] = jnp.concatenate(
        [rgd[c][0:2] for c in range(row)], axis=0
    )
    szo[2, :, 0:heads] = jnp.transpose(turn[...]).astype(BF16)
    keep(szo.at[:, mine, :], rzo.at[z], zo_recv)

    def send_zo(i):
        to = lax.rem(z + i, zs)
        send(szo.at[:, tokens_of(to), :], rzo.at[z], zo_send, zo_recv, at(r, to))

    loop(1, zs, send_zo)

    bytes_wait(rsy, sy_recv)
    total = rsy[0]
    for i in range(1, slabs):
        total = total + rsy[i]
    ssr[...] = total
    keep(ssr, rsr.at[r], sr_recv)

    def send_sr(i):
        send(ssr, rsr.at[r], sr_send, sr_recv, at(lax.rem(r + i, row), z))

    loop(1, row, send_sr)

    bytes_wait(ry, y_recv)

    def gate_back(d):
        inner_ref[1, :, lanes_of(d)] = (
            slope[:, lanes_of(d)] * ry[:, lanes_of(d)].astype(F32)
        ).astype(BF16)

    loop(0, row * zs, gate_back)
    bytes_wait(rdx, dx_recv)
    inner_ref[0] = rdx[...]

    bytes_wait(rzo, zo_recv)
    total = jnp.zeros((TOK, heads), F32)
    for k in range(zs):
        outer_ref[0, :, k * STATE : (k + 1) * STATE] = rzo[k, 0]
        outer_ref[1, :, k * STATE : (k + 1) * STATE] = rzo[k, 1]
        total = total + rzo[k, 2, :, 0:heads].astype(F32)
    gdt_ref[...] = total.astype(BF16)
    bytes_wait(rsr, sr_recv)
    total = rsr[0]
    for i in range(1, row):
        total = total + rsr[i]
    sums_ref[...] = total

    @pl.when(y < slabs - 1)
    def _():
        loop(0, slabs - 1 - y, lambda i: bytes_wait(ssend, s_send))

    @pl.when(y > 0)
    def _():
        loop(0, y, lambda i: bytes_wait(asend, a_send))

    blocks = sg.at[pl.ds(0, row * zs - 1)]
    for sem in (x_send, g_send, y_send, dx_send):
        bytes_wait(blocks, sem)
    others = pl.ds(0, row - 1)
    bytes_wait(sbc.at[pl.ds(0, zs - 1)], zb_send)
    bytes_wait(rb.at[others], b_send)
    bytes_wait(rc.at[others], c_send)
    bytes_wait(sdt.at[others], dt_send)
    bytes_wait(rdb.at[others], db_send)
    bytes_wait(rdc.at[others], dc_send)
    bytes_wait(sgd.at[others], gd_send)
    bytes_wait(rzo.at[pl.ds(0, zs - 1)], zo_send)
    bytes_wait(rsy.at[pl.ds(0, slabs - 1)], sy_send)
    bytes_wait(rsr.at[others], sr_send)


def unpack(
    inner_hbm, outer_hbm, dt_hbm, sums_ref,
    gx_ref, gz_ref, gb_ref, gc_ref, gdt_ref, bias_ref, alog_ref, skip_ref,
    inner, outer, dts, come, go,
):
    moves = (
        (inner_hbm.at[0], inner.at[0], gx_ref),
        (inner_hbm.at[1], inner.at[1], gz_ref),
        (outer_hbm.at[0], outer.at[0], gb_ref),
        (outer_hbm.at[1], outer.at[1], gc_ref),
        (dt_hbm, dts, gdt_ref),
    )
    came = [pltpu.make_async_copy(a, b, come.at[i]) for i, (a, b, _) in enumerate(moves)]
    gone = [pltpu.make_async_copy(b, c, go.at[i]) for i, (_, b, c) in enumerate(moves)]
    for copy in came:
        copy.start()
    for q, ref in enumerate((bias_ref, alog_ref, skip_ref)):
        ref[...] = sums_ref[q, 0 : ref.shape[0]]
    for first, second in zip(came, gone):
        first.wait()
        second.start()
    for copy in gone:
        copy.wait()


def shards(row, x_proj, z_gate, out_grad, b_proj, c_proj, dt_raw, dt_bias, a_log, d_skip):
    zs = lax.axis_size("head")
    slabs = lax.axis_size("seq") // row
    heads = 2 * row * zs
    length = zs * TOK
    inner = heads * HALF

    def vmem(*shape, dtype=BF16):
        return pltpu.VMEM(shape, dtype)

    square = (row, length, LANES)
    states = (row, STATE, LANES)
    per = 2 * row
    scratch = [
        vmem(TOK, inner),
        vmem(TOK, inner),
        vmem(TOK, inner),
        vmem(TOK, zs * STATE),
        vmem(TOK, zs * STATE),
        vmem(TOK, heads),
        pltpu.SMEM((per,), F32),
        pltpu.SMEM((per,), F32),
        pltpu.SMEM((per,), F32),
        vmem(row * zs, TOK, LANES),
        vmem(*square),
        vmem(*square),
        vmem(zs, 3, TOK, STATE),
        vmem(3, length, STATE),
        vmem(*square),
        vmem(*square),
        vmem(row, 8, length, dtype=F32),
        vmem(row, 8, length, dtype=F32),
        vmem(STATE + 16, LANES),
        vmem(STATE + 16, LANES),
        vmem(slabs, STATE + 16, LANES),
        vmem(slabs, STATE + 16, LANES),
        vmem(*square),
        vmem(*square),
        vmem(TOK, inner),
        vmem(TOK, inner),
        vmem(*square),
        vmem(*square),
        vmem(*square),
        vmem(*square),
        vmem(row, 8, length, dtype=F32),
        vmem(row, 8, length, dtype=F32),
        vmem(3, length, STATE),
        vmem(zs, 3, TOK, STATE),
        vmem(8, LANES, dtype=F32),
        vmem(slabs, 8, LANES, dtype=F32),
        vmem(8, LANES, dtype=F32),
        vmem(row, 8, LANES, dtype=F32),
        vmem(TOK, inner, dtype=F32),
        vmem(heads, length, dtype=F32),
        vmem(row, length, 8, dtype=F32),
        vmem(*square, dtype=F32),
        vmem(*square, dtype=F32),
        vmem(*square),
        vmem(*square),
        vmem(*states, dtype=F32),
        vmem(*states, dtype=F32),
        vmem(*states),
        vmem(row, length, length, dtype=F32),
        vmem(row, 2, length, length, dtype=F32),
        vmem(row, 2, length, length),
        vmem(*square, dtype=F32),
        vmem(*square, dtype=F32),
        vmem(*square, dtype=F32),
        vmem(row, 8, length, dtype=F32),
        vmem(row, 8, length, dtype=F32),
        vmem(row, 8, length, dtype=F32),
        vmem(row, 8, length, dtype=F32),
        vmem(row, 8, length, dtype=F32),
        vmem(1, LANES, dtype=F32),
    ]
    one, many = pltpu.SemaphoreType.DMA, lambda n: pltpu.SemaphoreType.DMA((n,))
    semaphores = [
        one, one,
        one, many(row),
        one, many(row),
        one, many(row),
        one, many(row),
        one, many(row),
        one, many(slabs),
        one, many(slabs),
        one, one,
        one, one,
        one, many(row),
        one, many(row),
        one, many(row),
        one, one,
        one, one,
        one, one,
        many(9),
    ]
    in_vmem = pl.BlockSpec(memory_space=pltpu.VMEM)
    in_hbm = pl.BlockSpec(memory_space=pltpu.HBM)
    like = jax.ShapeDtypeStruct
    results = pl.pallas_call(
        functools.partial(kernel, (slabs, row, zs, heads)),
        out_shape=[
            like((2, TOK, inner), BF16),
            like((2, TOK, zs * STATE), BF16),
            like((TOK, heads), BF16),
            like((8, LANES), F32),
        ],
        in_specs=[in_hbm] * 9,
        out_specs=[in_vmem] * 4,
        scratch_shapes=scratch + semaphores,
        compiler_params=pltpu.CompilerParams(
            collective_id=0, has_side_effects=True, vmem_limit_bytes=62 * 2**20
        ),
        name="scan_backward",
    )(x_proj, z_gate, out_grad, b_proj, c_proj, dt_raw, dt_bias, a_log, d_skip)
    anywhere = pl.BlockSpec(memory_space=pl.ANY)
    return pl.pallas_call(
        unpack,
        out_shape=[
            like((TOK, inner), BF16),
            like((TOK, inner), BF16),
            like((TOK, zs * STATE), BF16),
            like((TOK, zs * STATE), BF16),
            like((TOK, heads), BF16),
            like((per,), F32),
            like((per,), F32),
            like((per,), F32),
        ],
        in_specs=[anywhere] * 3 + [in_vmem],
        out_specs=[anywhere] * 5 + [in_vmem] * 3,
        scratch_shapes=[
            vmem(2, TOK, inner),
            vmem(2, TOK, zs * STATE),
            vmem(TOK, heads),
            many(5),
            many(5),
        ],
        compiler_params=pltpu.CompilerParams(vmem_limit_bytes=62 * 2**20),
        name="unpack",
    )(*results)


def solution(mesh, row=ROW):
    tokens = P(("seq", "head"), None)
    return jax.shard_map(
        functools.partial(shards, row),
        mesh=mesh,
        in_specs=(tokens,) * 6 + (P("head"),) * 3,
        out_specs=(tokens,) * 5 + (P("head"),) * 3,
        check_vma=False,
    )
```

time: 82.8 us -> 68.2 us (0.82)
  local copies, waits for them, and re-layouts: 10.8 us -> 0 us
  Pallas kernels: 71 us -> 67 us
    unnamed x23 -> x0, local copies, waits for them, and re-layouts: 10.2 us -> none
    pallas_call x1, Pallas kernels: 71 us -> 64 us  [shards(): pl.pallas_call(functools.partial(kernel, (slabs, row, zs, heads)), out_sh...]
    pallas_call x0 -> x1, Pallas kernels: none -> 3.02 us  [shards(): pl.pallas_call(unpack, out_shape=[like((TOK, inner), BF16), like((TOK, in...]
where the time goes in v2:
time: 68.2 us; the launch traced here: 67.6 us
  Pallas kernels  67 us (98%)
    pallas_call x1, Pallas kernels, shards(): pl.pallas_call(functools.partial(kernel, (slabs, row, zs, heads)), out_sh...  64 us
    pallas_call x1, Pallas kernels, shards(): pl.pallas_call(unpack, out_shape=[like((TOK, inner), BF16), like((TOK, in...  3.02 us

profile of v2, /device:TPU:1, one launch (start us, length us, event | category | flops | bytes accessed | tf_op | source)
XLA Modules:
  0.0 67.6 jit_solution(7833385741463831673)
XLA Ops:
  0.6 64.0 %scan_backward.1 = (bf16[2,16,8192]{2,1,0:T(8,128)(2,1)}, bf16[2,16,1024]{2,1,0:T(8,128)(2,1)}, bf16[16,128]{1,0:T(8,128)(2,1)}, f32[8,128]{1,0:T(8,128)}) custom-call(bf16[16,8192]{1,0:T(8,128)(2,1)} %x_hbm.1, bf16[16,8192]{1,0:T(8,128)(2,1)} %z_hbm.1, bf16[16,8192]{1,0:T(8,128)(2,1)} %og_hbm.1, bf16[16,1024]{1,0:T(8,128)(2,1)} %b_hbm.1, ...), custom_call_target="tpu_custom_call" | custom-call | tf_op jit(solution)/shard_map/scan_backward/pallas_call | solution.py:696
  64.6 3.0 %unpack.1 = (bf16[16,8192]{1,0:T(8,128)(2,1)}, bf16[16,8192]{1,0:T(8,128)(2,1)}, bf16[16,1024]{1,0:T(8,128)(2,1)}, bf16[16,1024]{1,0:T(8,128)(2,1)}, bf16[16,128...) custom-call(bf16[2,16,8192]{2,1,0:T(8,128)(2,1)} %get-tuple-element.12.inner_hbm, ...), custom_call_target="tpu_custom_call" | custom-call | tf_op jit(solution)/shard_map/unpack/pallas_call | solution.py:713

commit v3 on v2

--- a/solution.py
+++ b/solution.py
@@ -9,10 +9,12 @@
 
 ROW = 8
 TOK = 16
+WIDE = 2
+FIRST = 2
 STATE = 128
 LANES = 128
 HALF = 64
-AHEAD = 4
+AHEAD = 8
 
 F32 = jnp.float32
 BF16 = jnp.bfloat16
@@ -41,6 +43,17 @@
     lax.fori_loop(low, high, step, 0)
 
 
+def pairs(count, body, after=None):
+    def step(k):
+        for i in range(WIDE):
+            body(k * WIDE + i)
+        if after is not None:
+            for i in range(WIDE):
+                after(k * WIDE + i)
+
+    loop(0, count // WIDE, step)
+
+
 def bytes_wait(ref, sem):
     pltpu.make_async_copy(ref, ref, sem).wait()
 
@@ -50,13 +63,13 @@
     x_hbm, z_hbm, og_hbm, b_hbm, c_hbm, dt_hbm, bias_hbm, alog_hbm, skip_hbm,
     inner_ref, outer_ref, gdt_ref, sums_ref,
     x_ref, z_ref, og_ref, b_ref, c_ref, dt_ref, bias_ref, alog_ref, skip_ref,
-    sg, rx, rg, sbc, rzb, rb, rc, sdt, rdt, ssend, asend, srecv, arecv, sy, sdx, ry, rdx,
-    sdb, sdc, rdb, rdc, sgd, rgd, szo, rzo, ssy, rsy, ssr, rsr,
+    sx, sg, rx, rg, sbc, rzb, scz, rcz, rb, rc, sdt, rdt, ssend, asend, srecv, arecv, skept, rkept, fades, sy, sdx, ry, rdx,
+    sdb, sdc, rdb, rdc, sgd, rgd, szo, rzo, szc, rzc, ssy, rsy, ssr, rsr,
     slope, turn, cols, ecol, wcol, eg, wx, st_s, st_a, hb, affs, decs, scores,
     y_in, dx_in, db_in, ds0, dla0, rho, kap, cterm, skipsum,
-    zb_send, zb_recv, x_send, x_recv, g_send, g_recv, b_send, b_recv, c_send, c_recv,
-    dt_send, dt_recv, s_send, s_recv, a_send, a_recv, y_send, y_recv, dx_send, dx_recv,
-    db_send, db_recv, dc_send, dc_recv, gd_send, gd_recv, zo_send, zo_recv,
+    zb_send, zb_recv, zc_send, zc_recv, x_send, x_recv, g_send, g_recv, b_send, b_recv, c_send, c_recv,
+    dt_send, dt_recv, s_send, s_recv, a_send, a_recv, k_send, k_recv, y_send, y_recv, dx_send, dx_recv,
+    db_send, db_recv, dc_send, dc_recv, gd_send, gd_recv, zo_send, zo_recv, oc_send, oc_recv,
     sy_send, sy_recv, sr_send, sr_recv, load,
 ):
     slabs, row, zs, heads = sizes
@@ -90,6 +103,18 @@
 
     def keep(src, dst, recv_sem):
         pltpu.make_async_copy(src, dst, recv_sem).start()
+
+    barrier = pltpu.get_barrier_semaphore()
+
+    def greet(i):
+        pl.semaphore_signal(barrier, inc=1, device_id=at(*other(i)), device_id_type=MESH)
+
+    def greet_slab(i):
+        there = (lax.rem(y + i, slabs) * row + r, z)
+        pl.semaphore_signal(barrier, inc=1, device_id=there, device_id_type=MESH)
+
+    loop(1, row * zs, greet)
+    loop(1, slabs, greet_slab)
 
     loads = [
         pltpu.make_async_copy(there, here, load.at[i])
@@ -110,25 +135,15 @@
     for copy in loads:
         copy.start()
 
-    barrier = pltpu.get_barrier_semaphore()
-
-    def greet(i):
-        pl.semaphore_signal(barrier, inc=1, device_id=at(*other(i)), device_id_type=MESH)
-
-    def greet_slab(i):
-        there = (lax.rem(y + i, slabs) * row + r, z)
-        pl.semaphore_signal(barrier, inc=1, device_id=there, device_id_type=MESH)
-
-    loop(1, row * zs, greet)
-    loop(1, slabs, greet_slab)
-
     for copy in loads[:3]:
         copy.wait()
     for k in range(zs):
         sbc[k, 0] = b_ref[:, k * STATE : (k + 1) * STATE]
-        sbc[k, 1] = c_ref[:, k * STATE : (k + 1) * STATE]
-        sbc[k, 2, :, 0:heads] = dt_ref[...]
+        sbc[k, 1, :, 0:heads] = dt_ref[...]
+        scz[k] = c_ref[:, k * STATE : (k + 1) * STATE]
     loads[3].wait()
+    for d in range(row * zs):
+        sx[d] = x_ref[:, d * LANES : (d + 1) * LANES]
     pl.semaphore_wait(barrier, row * zs - 1 + slabs - 1)
 
     keep(sbc.at[z], rzb.at[:, mine, :], zb_recv)
@@ -139,12 +154,12 @@
 
     loop(1, zs, send_zb)
 
-    keep(x_ref.at[:, lanes_of(z * row + r)], rx.at[r, mine, :], x_recv.at[r])
+    keep(sx.at[z * row + r], rx.at[r, mine, :], x_recv.at[r])
 
     def send_x(i):
         r_to, z_to = other(i)
         send(
-            x_ref.at[:, lanes_of(z_to * row + r_to)],
+            sx.at[z_to * row + r_to],
             rx.at[r, mine, :],
             x_send,
             x_recv.at[r],
@@ -153,9 +168,16 @@
 
     loop(1, AHEAD * zs, send_x)
 
+    keep(scz.at[z], rcz.at[mine, :], zc_recv)
+
+    def send_zc(i):
+        to = lax.rem(z + i, zs)
+        send(scz.at[to], rcz.at[mine, :], zc_send, zc_recv, at(r, to))
+
+    loop(1, zs, send_zc)
+
     bytes_wait(rzb, zb_recv)
     keep(rzb.at[0], rb.at[r], b_recv.at[r])
-    keep(rzb.at[1], rc.at[r], c_recv.at[r])
 
     def send_b(i):
         to = lax.rem(r + i, row)
@@ -163,9 +185,11 @@
 
     loop(1, row, send_b)
 
+    loop(AHEAD * zs, row * zs, send_x)
+
     for copy in loads[4:]:
         copy.wait()
-    turn[...] = jnp.transpose(rzb[2].astype(F32)[:, 0:heads])
+    turn[...] = jnp.transpose(rzb[1].astype(F32)[:, 0:heads])
     raw = turn[pl.ds(pl.multiple_of(z * per, per), per), :]
     head_at = lax.broadcasted_iota(jnp.int32, (per, length), 0)
     token_at = lax.broadcasted_iota(jnp.int32, (per, length), 1)
@@ -193,30 +217,32 @@
         send(sdt.at[to], rdt.at[r], dt_send, dt_recv.at[r], at(to, z))
 
     loop(1, row, send_dt)
-    loop(AHEAD * zs, row * zs, send_x)
+
+    def gate(k):
+        for i in range(row):
+            d = k * row + i
+            zf, of = z_ref[:, lanes_of(d)].astype(F32), og_ref[:, lanes_of(d)].astype(F32)
+            s = jax.nn.sigmoid(zf)
+            sg[d] = (of * (zf * s)).astype(BF16)
+            slope[d] = of * (s * (1.0 + zf * (1.0 - s)))
+
+    loop(0, zs, gate)
+    keep(sg.at[z * row + r], rg.at[r, mine, :], g_recv.at[r])
+
+    def send_g(i):
+        r_to, z_to = other(i)
+        send(sg.at[z_to * row + r_to], rg.at[r, mine, :], g_send, g_recv.at[r], at(r_to, z_to))
+
+    loop(1, row * zs, send_g)
+
+    bytes_wait(rcz, zc_recv)
+    keep(rcz, rc.at[r], c_recv.at[r])
 
     def send_c(i):
         to = lax.rem(r + i, row)
-        send(rzb.at[1], rc.at[r], c_send, c_recv.at[r], at(to, z))
+        send(rcz, rc.at[r], c_send, c_recv.at[r], at(to, z))
 
     loop(1, row, send_c)
-
-    def gate(d):
-        zf, of = z_ref[:, lanes_of(d)].astype(F32), og_ref[:, lanes_of(d)].astype(F32)
-        s = jax.nn.sigmoid(zf)
-        sg[d] = (of * (zf * s)).astype(BF16)
-        slope[:, lanes_of(d)] = of * (s * (1.0 + zf * (1.0 - s)))
-
-    gate(z * row + r)
-    keep(sg.at[z * row + r], rg.at[r, mine, :], g_recv.at[r])
-
-    def send_g(i):
-        r_to, z_to = other(i)
-        d = z_to * row + r_to
-        gate(d)
-        send(sg.at[d], rg.at[r, mine, :], g_send, g_recv.at[r], at(r_to, z_to))
-
-    loop(1, row * zs, send_g)
 
     lane = lax.broadcasted_iota(jnp.int32, (1, LANES), 1)
     first = lane < HALF
@@ -235,42 +261,46 @@
         return lax.rem(r + row - k, row)
 
     def last_decay(c):
-        rows = rdt[c]
-        return jnp.exp(jnp.where(first, rows[2:3, length - 1 :], rows[3:4, length - 1 :]))
-
-    def with_keep(total, keep_all):
-        high = keep_all.astype(BF16).astype(F32)
-        mid = (keep_all - high).astype(BF16).astype(F32)
-        low = keep_all - high - mid
-        tail = jnp.where(sel_at == 0, high, jnp.where(sel_at == 1, mid, low))
-        return jnp.concatenate([total.astype(BF16), tail.astype(BF16)], axis=0)
-
-    def states(k):
+        return fades[c, 0:1]
+
+    def decays_of(k):
         c = chunk(k)
-        bytes_wait(rdt.at[c], dt_recv.at[c])
         rows = rdt[c]
         across = jnp.transpose(rows)
         cols[c] = across
         up = jnp.where(first, across[:, 2:3], across[:, 3:4])
         end = jnp.where(first, rows[2:3, length - 1 :], rows[3:4, length - 1 :])
         size = jnp.where(first, across[:, 0:1], across[:, 1:2])
-        w = jnp.exp(end - up) * size
         ecol[c] = jnp.exp(up)
-        wcol[c] = w
+        wcol[c] = jnp.exp(end - up) * size
+        fades[c] = jnp.broadcast_to(jnp.exp(end), (8, LANES))
+
+    loop(0, row, lambda c: bytes_wait(rdt.at[c], dt_recv.at[c]))
+    pairs(row, decays_of)
+    kept = fades[0]
+    for c in range(1, row):
+        kept = kept * fades[c]
+    skept[...] = kept
+
+    def send_kept(i):
+        there = (lax.rem(y + i, slabs) * row + r, z)
+        send(skept, rkept.at[y], k_send, k_recv.at[y], there)
+
+    loop(1, slabs, send_kept)
+
+    def states(k):
+        c = chunk(k)
         bytes_wait(rb.at[c], b_recv.at[c])
         bytes_wait(rx.at[c], x_recv.at[c])
-        grown = (w * rx[c].astype(F32)).astype(BF16)
+        grown = (wcol[c] * rx[c].astype(F32)).astype(BF16)
         wx[c] = grown
         st_s[c] = mm(rb[c], grown, 0, 0)
 
     loop(0, row, states)
     state = jnp.zeros((STATE, LANES), F32)
-    keep_all = jnp.ones((1, LANES), F32)
     for c in range(row):
-        fade = last_decay(c)
-        keep_all = keep_all * fade
-        state = fade * state + st_s[c]
-    ssend[...] = with_keep(state, keep_all)
+        state = last_decay(c) * state + st_s[c]
+    ssend[...] = state.astype(BF16)
 
     def send_s(i):
         @pl.when(y + i < slabs)
@@ -281,7 +311,6 @@
 
     def scored(k):
         c = chunk(k)
-        bytes_wait(rc.at[c], c_recv.at[c])
         xf = rx[c].astype(F32)
         across = cols[c]
         aff = mm(rc[c], rb[c], 1, 1)
@@ -296,7 +325,8 @@
             y_sum = y_sum + mm(score, (xf * sel[j]).astype(BF16), 1, 0)
         y_in[c] = y_sum
 
-    loop(0, row, scored)
+    loop(0, row, lambda c: bytes_wait(rc.at[c], c_recv.at[c]))
+    pairs(row, scored)
 
     def cotangents(k):
         c = chunk(k)
@@ -309,7 +339,7 @@
     back = jnp.zeros((STATE, LANES), F32)
     for c in reversed(range(row)):
         back = last_decay(c) * back + st_a[c]
-    asend[...] = with_keep(back, keep_all)
+    asend[...] = back.astype(BF16)
 
     def send_a(i):
         @pl.when(y >= i)
@@ -318,8 +348,11 @@
 
     loop(1, slabs, send_a)
 
+    def await_kept(source):
+        bytes_wait(rkept.at[source], k_recv.at[source])
+
+    loop(1, slabs, lambda i: await_kept(lax.rem(y + i, slabs)))
     state = jnp.zeros((STATE, LANES), F32)
-    srecv[y] = ssend[...]
     for i in reversed(range(1, slabs)):
         source = lax.rem(y + slabs - i, slabs)
 
@@ -327,30 +360,29 @@
         def _():
             bytes_wait(srecv.at[source], s_recv.at[source])
 
-        ends = srecv[source, STATE : STATE + 16].astype(F32)
-        fade = ends[0:1] + ends[1:2] + ends[2:3]
-        state = jnp.where(y >= i, fade * state + srecv[source, 0:STATE].astype(F32), state)
+        fade = rkept[source, 0:1]
+        state = jnp.where(y >= i, fade * state + srecv[source].astype(F32), state)
     for c in range(row):
         hb[c] = state.astype(BF16)
         here = st_s[c]
         st_s[c] = state
         state = last_decay(c) * state + here
 
-    there = lanes_of(z * row + r)
+    there = z * row + r
 
     def leave(buffer, k, c, landing, send_sem, recv_sem):
         @pl.when(k == 0)
         def _():
-            keep(buffer.at[c, mine, :], landing.at[:, there], recv_sem)
+            keep(buffer.at[c, mine, :], landing.at[there], recv_sem)
 
         @pl.when(k > 0)
         def _():
-            send(buffer.at[c, mine, :], landing.at[:, there], send_sem, recv_sem, at(c, z))
+            send(buffer.at[c, mine, :], landing.at[there], send_sem, recv_sem, at(c, z))
 
         def one(i):
             to = lax.rem(z + i, zs)
             part = buffer.at[c, tokens_of(to), :]
-            send(part, landing.at[:, there], send_sem, recv_sem, at(c, to))
+            send(part, landing.at[there], send_sem, recv_sem, at(c, to))
 
         loop(1, zs, one)
 
@@ -358,12 +390,12 @@
         c = lax.rem(r + k, row)
         yi = ecol[c] * mm(rc[c], hb[c], 1, 0)
         sy[c] = (y_in[c] + yi).astype(BF16)
-        leave(sy, k, c, ry, y_send, y_recv)
         rho[c] = mm(pick16, (rg[c].astype(F32) * yi).astype(BF16), 1, 1)[0:8]
 
-    loop(0, row, finish_y)
-
-    skipsum[...] = jnp.zeros_like(skipsum)
+    def leave_y(k):
+        leave(sy, k, lax.rem(r + k, row), ry, y_send, y_recv)
+
+    pairs(row, finish_y, leave_y)
 
     def pulled(k):
         c = lax.rem(r + k, row)
@@ -388,7 +420,10 @@
         dx_in[c] = dx_sum
         sdc[c] = (mm(pulls, bs, 1, 0) + mm(eg[c], hb[c], 1, 1)).astype(BF16)
         db_in[c] = mm(pulls, cs, 0, 0)
-        skipsum[...] = skipsum[...] + jnp.sum(xf * gf, axis=0, keepdims=True)
+        skipsum[pl.ds(c, 1), :] = jnp.sum(xf * gf, axis=0, keepdims=True)
+
+    def leave_c(k):
+        c = lax.rem(r + k, row)
 
         @pl.when(k == 0)
         def _():
@@ -398,10 +433,9 @@
         def _():
             send(sdc.at[c], rdc.at[r], dc_send, dc_recv.at[r], at(c, z))
 
-    loop(0, row, pulled)
+    pairs(row, pulled, leave_c)
 
     back = jnp.zeros((STATE, LANES), F32)
-    arecv[y] = asend[...]
     for i in reversed(range(1, slabs)):
         source = lax.rem(y + i, slabs)
 
@@ -409,9 +443,7 @@
         def _():
             bytes_wait(arecv.at[source], a_recv.at[source])
 
-        ends = arecv[source, STATE : STATE + 16].astype(F32)
-        fade = ends[0:1] + ends[1:2] + ends[2:3]
-        part = arecv[source, 0:STATE].astype(F32)
+        fade, part = rkept[source, 0:1], arecv[source].astype(F32)
         back = jnp.where(y + i < slabs, fade * back + part, back)
     for c in reversed(range(row)):
         hb[c] = back.astype(BF16)
@@ -426,8 +458,14 @@
         c = lax.rem(r + k, row)
         bi = wcol[c] * mm(rb[c], hb[c], 1, 0)
         sdx[c] = (dx_in[c] + bi).astype(BF16)
-        leave(sdx, k, c, rdx, dx_send, dx_recv)
         sdb[c] = (db_in[c] + mm(wx[c], hb[c], 1, 1)).astype(BF16)
+        kap[c] = mm(pick16, (rx[c].astype(F32) * bi).astype(BF16), 1, 1)[0:8]
+
+    def leave_x(k):
+        leave(sdx, k, lax.rem(r + k, row), rdx, dx_send, dx_recv)
+
+    def leave_b(k):
+        c = lax.rem(r + k, row)
 
         @pl.when(k == 0)
         def _():
@@ -437,9 +475,24 @@
         def _():
             send(sdb.at[c], rdb.at[r], db_send, db_recv.at[r], at(c, z))
 
-        kap[c] = mm(pick16, (rx[c].astype(F32) * bi).astype(BF16), 1, 1)[0:8]
-
-    loop(0, row, finish_x)
+        @pl.when(k < FIRST)
+        def _():
+            leave_x(k)
+
+    pairs(row, finish_x, leave_b)
+
+    loop(0, row, lambda c: bytes_wait(rdc.at[c], dc_recv.at[c]))
+    total = rdc[0].astype(F32)
+    for c in range(1, row):
+        total = total + rdc[c].astype(F32)
+    szc[...] = total.astype(BF16)
+    keep(szc.at[mine, :], rzc.at[z], oc_recv)
+
+    def send_oc(i):
+        to = lax.rem(z + i, zs)
+        send(szc.at[tokens_of(to), :], rzc.at[z], oc_send, oc_recv, at(r, to))
+
+    loop(1, zs, send_oc)
 
     flat = (row * 8, length)
     dla = (
@@ -485,12 +538,8 @@
         send(ssy, rsy.at[y], sy_send, sy_recv, (lax.rem(y + i, slabs) * row + r, z))
 
     loop(1, slabs, send_sy)
-
-    loop(0, row, lambda c: bytes_wait(rdc.at[c], dc_recv.at[c]))
-    total = rdc[0].astype(F32)
-    for c in range(1, row):
-        total = total + rdc[c].astype(F32)
-    szo[1] = total.astype(BF16)
+    loop(FIRST, row, leave_x)
+
     loop(0, row, lambda c: bytes_wait(rdb.at[c], db_recv.at[c]))
     total = rdb[0].astype(F32)
     for c in range(1, row):
@@ -501,7 +550,7 @@
     turn[pl.ds(pl.multiple_of(z * per, per), per), :] = jnp.concatenate(
         [rgd[c][0:2] for c in range(row)], axis=0
     )
-    szo[2, :, 0:heads] = jnp.transpose(turn[...]).astype(BF16)
+    szo[1, :, 0:heads] = jnp.transpose(turn[...]).astype(BF16)
     keep(szo.at[:, mine, :], rzo.at[z], zo_recv)
 
     def send_zo(i):
@@ -524,21 +573,24 @@
 
     bytes_wait(ry, y_recv)
 
-    def gate_back(d):
-        inner_ref[1, :, lanes_of(d)] = (
-            slope[:, lanes_of(d)] * ry[:, lanes_of(d)].astype(F32)
-        ).astype(BF16)
-
-    loop(0, row * zs, gate_back)
+    def gate_back(k):
+        for i in range(row):
+            d = k * row + i
+            inner_ref[1, :, lanes_of(d)] = (slope[d] * ry[d].astype(F32)).astype(BF16)
+
+    loop(0, zs, gate_back)
+    bytes_wait(rzc, oc_recv)
+    for k in range(zs):
+        outer_ref[1, :, k * STATE : (k + 1) * STATE] = rzc[k]
     bytes_wait(rdx, dx_recv)
-    inner_ref[0] = rdx[...]
+    for d in range(row * zs):
+        inner_ref[0, :, d * LANES : (d + 1) * LANES] = rdx[d]
 
     bytes_wait(rzo, zo_recv)
     total = jnp.zeros((TOK, heads), F32)
     for k in range(zs):
         outer_ref[0, :, k * STATE : (k + 1) * STATE] = rzo[k, 0]
-        outer_ref[1, :, k * STATE : (k + 1) * STATE] = rzo[k, 1]
-        total = total + rzo[k, 2, :, 0:heads].astype(F32)
+        total = total + rzo[k, 1, :, 0:heads].astype(F32)
     gdt_ref[...] = total.astype(BF16)
     bytes_wait(rsr, sr_recv)
     total = rsr[0]
@@ -559,6 +611,7 @@
         bytes_wait(blocks, sem)
     others = pl.ds(0, row - 1)
     bytes_wait(sbc.at[pl.ds(0, zs - 1)], zb_send)
+    bytes_wait(scz.at[pl.ds(0, zs - 1)], zc_send)
     bytes_wait(rb.at[others], b_send)
     bytes_wait(rc.at[others], c_send)
     bytes_wait(sdt.at[others], dt_send)
@@ -566,8 +619,10 @@
     bytes_wait(rdc.at[others], dc_send)
     bytes_wait(sgd.at[others], gd_send)
     bytes_wait(rzo.at[pl.ds(0, zs - 1)], zo_send)
+    bytes_wait(rzc.at[pl.ds(0, zs - 1)], oc_send)
     bytes_wait(rsy.at[pl.ds(0, slabs - 1)], sy_send)
     bytes_wait(rsr.at[others], sr_send)
+    bytes_wait(rkept.at[pl.ds(0, slabs - 1)], k_send)
 
 
 def unpack(
@@ -619,35 +674,43 @@
         pltpu.SMEM((per,), F32),
         pltpu.SMEM((per,), F32),
         vmem(row * zs, TOK, LANES),
-        vmem(*square),
-        vmem(*square),
-        vmem(zs, 3, TOK, STATE),
-        vmem(3, length, STATE),
+        vmem(row * zs, TOK, LANES),
+        vmem(*square),
+        vmem(*square),
+        vmem(zs, 2, TOK, STATE),
+        vmem(2, length, STATE),
+        vmem(zs, TOK, STATE),
+        vmem(length, STATE),
         vmem(*square),
         vmem(*square),
         vmem(row, 8, length, dtype=F32),
         vmem(row, 8, length, dtype=F32),
-        vmem(STATE + 16, LANES),
-        vmem(STATE + 16, LANES),
-        vmem(slabs, STATE + 16, LANES),
-        vmem(slabs, STATE + 16, LANES),
-        vmem(*square),
-        vmem(*square),
-        vmem(TOK, inner),
-        vmem(TOK, inner),
+        vmem(STATE, LANES),
+        vmem(STATE, LANES),
+        vmem(slabs, STATE, LANES),
+        vmem(slabs, STATE, LANES),
+        vmem(8, LANES, dtype=F32),
+        vmem(slabs, 8, LANES, dtype=F32),
+        vmem(row, 8, LANES, dtype=F32),
+        vmem(*square),
+        vmem(*square),
+        vmem(row * zs, TOK, LANES),
+        vmem(row * zs, TOK, LANES),
         vmem(*square),
         vmem(*square),
         vmem(*square),
         vmem(*square),
         vmem(row, 8, length, dtype=F32),
         vmem(row, 8, length, dtype=F32),
-        vmem(3, length, STATE),
-        vmem(zs, 3, TOK, STATE),
+        vmem(2, length, STATE),
+        vmem(zs, 2, TOK, STATE),
+        vmem(length, STATE),
+        vmem(zs, TOK, STATE),
         vmem(8, LANES, dtype=F32),
         vmem(slabs, 8, LANES, dtype=F32),
         vmem(8, LANES, dtype=F32),
         vmem(row, 8, LANES, dtype=F32),
-        vmem(TOK, inner, dtype=F32),
+        vmem(row * zs, TOK, LANES, dtype=F32),
         vmem(heads, length, dtype=F32),
         vmem(row, length, 8, dtype=F32),
         vmem(*square, dtype=F32),
@@ -668,10 +731,11 @@
         vmem(row, 8, length, dtype=F32),
         vmem(row, 8, length, dtype=F32),
         vmem(row, 8, length, dtype=F32),
-        vmem(1, LANES, dtype=F32),
+        vmem(row, LANES, dtype=F32),
     ]
     one, many = pltpu.SemaphoreType.DMA, lambda n: pltpu.SemaphoreType.DMA((n,))
     semaphores = [
+        one, one,
         one, one,
         one, many(row),
         one, many(row),
@@ -680,11 +744,13 @@
         one, many(row),
         one, many(slabs),
         one, many(slabs),
+        one, many(slabs),
         one, one,
         one, one,
         one, many(row),
         one, many(row),
         one, many(row),
+        one, one,
         one, one,
         one, one,
         one, one,

time: 68.2 us -> 65.3 us (0.957)
  Pallas kernels: 67 us -> 64.5 us
    pallas_call x1, Pallas kernels: 64 us -> 61.4 us  [shards(): pl.pallas_call(functools.partial(kernel, (slabs, row, zs, heads)), out_sh...]
where the time goes in v3:
time: 65.3 us; the launch traced here: 65.1 us
  Pallas kernels  64.5 us (99%)
    pallas_call x1, Pallas kernels, shards(): pl.pallas_call(functools.partial(kernel, (slabs, row, zs, heads)), out_sh...  61.4 us
    pallas_call x1, Pallas kernels, shards(): pl.pallas_call(unpack, out_shape=[like((TOK, inner), BF16), like((TOK, in...  3.02 us

profile of v3, /device:TPU:1, one launch (start us, length us, event | category | flops | bytes accessed | tf_op | source)
XLA Modules:
  0.0 65.1 jit_solution(17779417124347206141)
XLA Ops:
  0.6 61.4 %scan_backward.1 = (bf16[2,16,8192]{2,1,0:T(8,128)(2,1)}, bf16[2,16,1024]{2,1,0:T(8,128)(2,1)}, bf16[16,128]{1,0:T(8,128)(2,1)}, f32[8,128]{1,0:T(8,128)}) custom-call(bf16[16,8192]{1,0:T(8,128)(2,1)} %x_hbm.1, bf16[16,8192]{1,0:T(8,128)(2,1)} %z_hbm.1, bf16[16,8192]{1,0:T(8,128)(2,1)} %og_hbm.1, bf16[16,1024]{1,0:T(8,128)(2,1)} %b_hbm.1, ...), custom_call_target="tpu_custom_call" | custom-call | tf_op jit(solution)/shard_map/scan_backward/pallas_call | solution.py:762
  62.1 3.0 %unpack.1 = (bf16[16,8192]{1,0:T(8,128)(2,1)}, bf16[16,8192]{1,0:T(8,128)(2,1)}, bf16[16,1024]{1,0:T(8,128)(2,1)}, bf16[16,1024]{1,0:T(8,128)(2,1)}, bf16[16,128...) custom-call(bf16[2,16,8192]{2,1,0:T(8,128)(2,1)} %get-tuple-element.12.inner_hbm, ...), custom_call_target="tpu_custom_call" | custom-call | tf_op jit(solution)/shard_map/unpack/pallas_call | solution.py:779

commit v4 on v3

--- a/solution.py
+++ b/solution.py
@@ -9,12 +9,11 @@
 
 ROW = 8
 TOK = 16
+PARTS = 4
 WIDE = 2
-FIRST = 2
 STATE = 128
 LANES = 128
 HALF = 64
-AHEAD = 8
 
 F32 = jnp.float32
 BF16 = jnp.bfloat16
@@ -61,23 +60,28 @@
 def kernel(
     sizes,
     x_hbm, z_hbm, og_hbm, b_hbm, c_hbm, dt_hbm, bias_hbm, alog_hbm, skip_hbm,
-    inner_ref, outer_ref, gdt_ref, sums_ref,
+    inner_hbm, outer_hbm, gdt_hbm, sums_hbm,
     x_ref, z_ref, og_ref, b_ref, c_ref, dt_ref, bias_ref, alog_ref, skip_ref,
     sx, sg, rx, rg, sbc, rzb, scz, rcz, rb, rc, sdt, rdt, ssend, asend, srecv, arecv, skept, rkept, fades, sy, sdx, ry, rdx,
-    sdb, sdc, rdb, rdc, sgd, rgd, szo, rzo, szc, rzc, ssy, rsy, ssr, rsr,
-    slope, turn, cols, ecol, wcol, eg, wx, st_s, st_a, hb, affs, decs, scores,
-    y_in, dx_in, db_in, ds0, dla0, rho, kap, cterm, skipsum,
+    sdb, sdc, mdb, mdc, tdb, tdc, rdb, rdc, sgd, rgd, szo, rzo, szc, rzc, ssy, rsy, ssr, rsr,
+    inner_ref, outer_ref, gdt_ref, sums_ref, slope, turn, cols, ecol, wcol, eg, wx, st_s, st_a, hb, gb, affs, decs, scores,
+    y_in, dx_in, dc_in, db_in, ds0, dla0, rho, kap, cterm, skipsum,
     zb_send, zb_recv, zc_send, zc_recv, x_send, x_recv, g_send, g_recv, b_send, b_recv, c_send, c_recv,
     dt_send, dt_recv, s_send, s_recv, a_send, a_recv, k_send, k_recv, y_send, y_recv, dx_send, dx_recv,
-    db_send, db_recv, dc_send, dc_recv, gd_send, gd_recv, zo_send, zo_recv, oc_send, oc_recv,
-    sy_send, sy_recv, sr_send, sr_recv, load,
+    db_send, db_recv, dc_send, dc_recv, mb_send, mb_recv, mc_send, mc_recv, gd_send, gd_recv, zo_send, zo_recv, oc_send, oc_recv,
+    sy_send, sy_recv, sr_send, sr_recv, load, done,
 ):
     slabs, row, zs, heads = sizes
     length = zs * TOK
     per = 2 * row
     seq, z = lax.axis_index("seq"), lax.axis_index("head")
     y, r = lax.div(seq, row), lax.rem(seq, row)
+    low = y < slabs // 2
     mine = pl.ds(pl.multiple_of(z * TOK, TOK), TOK)
+
+    def either(early, late):
+        pl.when(low)(early)
+        pl.when(jnp.logical_not(low))(late)
 
     def at(row_to, z_to):
         return (y * row + row_to, z_to)
@@ -137,10 +141,14 @@
 
     for copy in loads[:3]:
         copy.wait()
+    def pack(one_ref, two_ref):
+        for k in range(zs):
+            sbc[k, 0] = one_ref[:, k * STATE : (k + 1) * STATE]
+            scz[k] = two_ref[:, k * STATE : (k + 1) * STATE]
+
+    either(lambda: pack(b_ref, c_ref), lambda: pack(c_ref, b_ref))
     for k in range(zs):
-        sbc[k, 0] = b_ref[:, k * STATE : (k + 1) * STATE]
         sbc[k, 1, :, 0:heads] = dt_ref[...]
-        scz[k] = c_ref[:, k * STATE : (k + 1) * STATE]
     loads[3].wait()
     for d in range(row * zs):
         sx[d] = x_ref[:, d * LANES : (d + 1) * LANES]
@@ -154,19 +162,36 @@
 
     loop(1, zs, send_zb)
 
-    keep(sx.at[z * row + r], rx.at[r, mine, :], x_recv.at[r])
-
     def send_x(i):
         r_to, z_to = other(i)
-        send(
-            sx.at[z_to * row + r_to],
-            rx.at[r, mine, :],
-            x_send,
-            x_recv.at[r],
-            at(r_to, z_to),
-        )
-
-    loop(1, AHEAD * zs, send_x)
+        d = z_to * row + r_to
+        send(sx.at[d], rx.at[r, mine, :], x_send, x_recv.at[r], at(r_to, z_to))
+
+    def all_x():
+        keep(sx.at[z * row + r], rx.at[r, mine, :], x_recv.at[r])
+        loop(1, row * zs, send_x)
+
+    def gate(k):
+        for i in range(row):
+            d = k * row + i
+            zf, of = z_ref[:, lanes_of(d)].astype(F32), og_ref[:, lanes_of(d)].astype(F32)
+            s = jax.nn.sigmoid(zf)
+            sg[d] = (of * (zf * s)).astype(BF16)
+            slope[d] = of * (s * (1.0 + zf * (1.0 - s)))
+
+    def send_g(i):
+        r_to, z_to = other(i)
+        d = z_to * row + r_to
+        send(sg.at[d], rg.at[r, mine, :], g_send, g_recv.at[r], at(r_to, z_to))
+
+    def all_g():
+        for copy in loads[4:6]:
+            copy.wait()
+        loop(0, zs, gate)
+        keep(sg.at[z * row + r], rg.at[r, mine, :], g_recv.at[r])
+        loop(1, row * zs, send_g)
+
+    either(all_x, all_g)
 
     keep(scz.at[z], rcz.at[mine, :], zc_recv)
 
@@ -176,18 +201,21 @@
 
     loop(1, zs, send_zc)
 
+    def share(src, dst, send_sem, recv_sem):
+        keep(src, dst.at[r], recv_sem.at[r])
+
+        def one(i):
+            to = lax.rem(r + i, row)
+            send(src, dst.at[r], send_sem, recv_sem.at[r], at(to, z))
+
+        loop(1, row, one)
+
     bytes_wait(rzb, zb_recv)
-    keep(rzb.at[0], rb.at[r], b_recv.at[r])
-
-    def send_b(i):
-        to = lax.rem(r + i, row)
-        send(rzb.at[0], rb.at[r], b_send, b_recv.at[r], at(to, z))
-
-    loop(1, row, send_b)
-
-    loop(AHEAD * zs, row * zs, send_x)
-
-    for copy in loads[4:]:
+    either(
+        lambda: share(rzb.at[0], rb, b_send, b_recv), lambda: share(rzb.at[0], rc, c_send, c_recv)
+    )
+
+    for copy in loads[6:]:
         copy.wait()
     turn[...] = jnp.transpose(rzb[1].astype(F32)[:, 0:heads])
     raw = turn[pl.ds(pl.multiple_of(z * per, per), per), :]
@@ -218,31 +246,9 @@
 
     loop(1, row, send_dt)
 
-    def gate(k):
-        for i in range(row):
-            d = k * row + i
-            zf, of = z_ref[:, lanes_of(d)].astype(F32), og_ref[:, lanes_of(d)].astype(F32)
-            s = jax.nn.sigmoid(zf)
-            sg[d] = (of * (zf * s)).astype(BF16)
-            slope[d] = of * (s * (1.0 + zf * (1.0 - s)))
-
-    loop(0, zs, gate)
-    keep(sg.at[z * row + r], rg.at[r, mine, :], g_recv.at[r])
-
-    def send_g(i):
-        r_to, z_to = other(i)
-        send(sg.at[z_to * row + r_to], rg.at[r, mine, :], g_send, g_recv.at[r], at(r_to, z_to))
-
-    loop(1, row * zs, send_g)
-
+    either(all_g, all_x)
     bytes_wait(rcz, zc_recv)
-    keep(rcz, rc.at[r], c_recv.at[r])
-
-    def send_c(i):
-        to = lax.rem(r + i, row)
-        send(rcz, rc.at[r], c_send, c_recv.at[r], at(to, z))
-
-    loop(1, row, send_c)
+    either(lambda: share(rcz, rc, c_send, c_recv), lambda: share(rcz, rb, b_send, b_recv))
 
     lane = lax.broadcasted_iota(jnp.int32, (1, LANES), 1)
     first = lane < HALF
@@ -290,43 +296,27 @@
 
     def states(k):
         c = chunk(k)
-        bytes_wait(rb.at[c], b_recv.at[c])
         bytes_wait(rx.at[c], x_recv.at[c])
         grown = (wcol[c] * rx[c].astype(F32)).astype(BF16)
         wx[c] = grown
         st_s[c] = mm(rb[c], grown, 0, 0)
 
-    loop(0, row, states)
-    state = jnp.zeros((STATE, LANES), F32)
-    for c in range(row):
-        state = last_decay(c) * state + st_s[c]
-    ssend[...] = state.astype(BF16)
-
     def send_s(i):
         @pl.when(y + i < slabs)
         def _():
             send(ssend, srecv.at[y], s_send, s_recv.at[y], ((y + i) * row + r, z))
 
-    loop(1, slabs, send_s)
-
-    def scored(k):
-        c = chunk(k)
-        xf = rx[c].astype(F32)
-        across = cols[c]
-        aff = mm(rc[c], rb[c], 1, 1)
-        affs[c] = aff
-        y_sum = skip * xf
-        for j in range(2):
-            fall = across[:, 2 + j : 3 + j] - rdt[c, 2 + j : 3 + j, :]
-            e = jnp.where(causal, jnp.exp(fall), 0.0)
-            decs[c, j] = e
-            score = (e * aff * rdt[c, j : j + 1, :]).astype(BF16)
-            scores[c, j] = score
-            y_sum = y_sum + mm(score, (xf * sel[j]).astype(BF16), 1, 0)
-        y_in[c] = y_sum
-
-    loop(0, row, lambda c: bytes_wait(rc.at[c], c_recv.at[c]))
-    pairs(row, scored)
+    def states_out():
+        loop(0, row, lambda c: bytes_wait(rb.at[c], b_recv.at[c]))
+        states_late()
+
+    def states_late():
+        loop(0, row, states)
+        state = jnp.zeros((STATE, LANES), F32)
+        for c in range(row):
+            state = last_decay(c) * state + st_s[c]
+        ssend[...] = state.astype(BF16)
+        loop(1, slabs, send_s)
 
     def cotangents(k):
         c = chunk(k)
@@ -335,42 +325,95 @@
         eg[c] = faded
         st_a[c] = mm(rc[c], faded, 0, 0)
 
-    loop(0, row, cotangents)
-    back = jnp.zeros((STATE, LANES), F32)
-    for c in reversed(range(row)):
-        back = last_decay(c) * back + st_a[c]
-    asend[...] = back.astype(BF16)
-
     def send_a(i):
         @pl.when(y >= i)
         def _():
             send(asend, arecv.at[y], a_send, a_recv.at[y], ((y - i) * row + r, z))
 
-    loop(1, slabs, send_a)
-
-    def await_kept(source):
-        bytes_wait(rkept.at[source], k_recv.at[source])
-
-    loop(1, slabs, lambda i: await_kept(lax.rem(y + i, slabs)))
-    state = jnp.zeros((STATE, LANES), F32)
-    for i in reversed(range(1, slabs)):
-        source = lax.rem(y + slabs - i, slabs)
-
-        @pl.when(y >= i)
-        def _():
-            bytes_wait(srecv.at[source], s_recv.at[source])
-
-        fade = rkept[source, 0:1]
-        state = jnp.where(y >= i, fade * state + srecv[source].astype(F32), state)
-    for c in range(row):
-        hb[c] = state.astype(BF16)
-        here = st_s[c]
-        st_s[c] = state
-        state = last_decay(c) * state + here
+    def cotangents_out():
+        loop(0, row, lambda c: bytes_wait(rc.at[c], c_recv.at[c]))
+        cotangents_late()
+
+    def cotangents_late():
+        loop(0, row, cotangents)
+        back = jnp.zeros((STATE, LANES), F32)
+        for c in reversed(range(row)):
+            back = last_decay(c) * back + st_a[c]
+        asend[...] = back.astype(BF16)
+        loop(1, slabs, send_a)
+
+    def inner_y(c):
+        xf = rx[c].astype(F32)
+        total = skip * xf
+        for j in range(2):
+            total = total + mm(scores[c, j], (xf * sel[j]).astype(BF16), 1, 0)
+        y_in[c] = total
+
+    def inner_x(c):
+        gf = rg[c].astype(F32)
+        total = skip * gf
+        for j in range(2):
+            total = total + mm(scores[c, j], (gf * sel[j]).astype(BF16), 0, 0)
+        dx_in[c] = total
+
+    def scored(then, k):
+        c = chunk(k)
+        across = cols[c]
+        aff = mm(rc[c], rb[c], 1, 1)
+        affs[c] = aff
+        for j in range(2):
+            fall = across[:, 2 + j : 3 + j] - rdt[c, 2 + j : 3 + j, :]
+            e = jnp.where(causal, jnp.exp(fall), 0.0)
+            decs[c, j] = e
+            scores[c, j] = (e * aff * rdt[c, j : j + 1, :]).astype(BF16)
+        then(c)
+
+    def await_kept():
+        def one(i):
+            source = lax.rem(y + i, slabs)
+            bytes_wait(rkept.at[source], k_recv.at[source])
+
+        loop(1, slabs, one)
+
+    def states_in():
+        state = jnp.zeros((STATE, LANES), F32)
+        for i in reversed(range(1, slabs)):
+            source = lax.rem(y + slabs - i, slabs)
+
+            @pl.when(y >= i)
+            def _():
+                bytes_wait(srecv.at[source], s_recv.at[source])
+
+            fade = rkept[source, 0:1]
+            state = jnp.where(y >= i, fade * state + srecv[source].astype(F32), state)
+        for c in range(row):
+            hb[c] = state.astype(BF16)
+            here = st_s[c]
+            st_s[c] = state
+            state = last_decay(c) * state + here
+
+    def cotangents_in():
+        back = jnp.zeros((STATE, LANES), F32)
+        for i in reversed(range(1, slabs)):
+            source = lax.rem(y + i, slabs)
+
+            @pl.when(y + i < slabs)
+            def _():
+                bytes_wait(arecv.at[source], a_recv.at[source])
+
+            fade, part = rkept[source, 0:1], arecv[source].astype(F32)
+            back = jnp.where(y + i < slabs, fade * back + part, back)
+        for c in reversed(range(row)):
+            gb[c] = back.astype(BF16)
+            here = st_a[c]
+            st_a[c] = back
+            back = last_decay(c) * back + here
 
     there = z * row + r
 
-    def leave(buffer, k, c, landing, send_sem, recv_sem):
+    def leave(buffer, landing, send_sem, recv_sem, k):
+        c = lax.rem(r + k, row)
+
         @pl.when(k == 0)
         def _():
             keep(buffer.at[c, mine, :], landing.at[there], recv_sem)
@@ -385,6 +428,41 @@
             send(part, landing.at[there], send_sem, recv_sem, at(c, to))
 
         loop(1, zs, one)
+
+    leave_y = functools.partial(leave, sy, ry, y_send, y_recv)
+    leave_x = functools.partial(leave, sdx, rdx, dx_send, dx_recv)
+
+    half, mate = row // 2, lax.rem(r, 2)
+    chip = lax.div(r, 2)
+
+    def to_mate(buffer, landing, send_sem, recv_sem):
+        def one(i):
+            src = buffer.at[2 * i + 1 - mate]
+            send(src, landing.at[i], send_sem, recv_sem.at[i], at(r + 1 - 2 * mate, z))
+
+        loop(0, half, one)
+
+    def to_chips(buffer, landing, recv_sem, summed, final, out_sem, in_sem):
+        def one(k):
+            i = lax.rem(chip + k, half)
+            c = 2 * i + mate
+            bytes_wait(landing.at[i], recv_sem.at[i])
+            summed[i] = (buffer[c].astype(F32) + landing[i].astype(F32)).astype(BF16)
+
+            @pl.when(k == 0)
+            def _():
+                keep(summed.at[i], final.at[chip], in_sem.at[chip])
+
+            @pl.when(k > 0)
+            def _():
+                send(summed.at[i], final.at[chip], out_sem, in_sem.at[chip], at(c, z))
+
+        loop(0, half, one)
+
+    c_to_mate = functools.partial(to_mate, sdc, mdc, mc_send, mc_recv)
+    b_to_mate = functools.partial(to_mate, sdb, mdb, mb_send, mb_recv)
+    c_to_chips = functools.partial(to_chips, sdc, mdc, mc_recv, tdc, rdc, dc_send, dc_recv)
+    b_to_chips = functools.partial(to_chips, sdb, mdb, mb_recv, tdb, rdb, db_send, db_recv)
 
     def finish_y(k):
         c = lax.rem(r + k, row)
@@ -392,22 +470,29 @@
         sy[c] = (y_in[c] + yi).astype(BF16)
         rho[c] = mm(pick16, (rg[c].astype(F32) * yi).astype(BF16), 1, 1)[0:8]
 
-    def leave_y(k):
-        leave(sy, k, lax.rem(r + k, row), ry, y_send, y_recv)
-
-    pairs(row, finish_y, leave_y)
-
-    def pulled(k):
+    def finish_x(k):
         c = lax.rem(r + k, row)
-        xs, gs, bs, cs = rx[c], rg[c], rb[c], rc[c]
+        bi = wcol[c] * mm(rb[c], gb[c], 1, 0)
+        sdx[c] = (dx_in[c] + bi).astype(BF16)
+        kap[c] = mm(pick16, (rx[c].astype(F32) * bi).astype(BF16), 1, 1)[0:8]
+
+    def finish_c(k):
+        c = lax.rem(r + k, row)
+        sdc[c] = (dc_in[c] + mm(eg[c], hb[c], 1, 1)).astype(BF16)
+
+    def finish_b(k):
+        c = lax.rem(r + k, row)
+        sdb[c] = (db_in[c] + mm(wx[c], gb[c], 1, 1)).astype(BF16)
+
+    def pulled(then, k):
+        c = lax.rem(r + k, row)
+        xs, gs = rx[c], rg[c]
         xf, gf = xs.astype(F32), gs.astype(F32)
         aff = affs[c]
-        dx_sum = skip * gf
         pulls = jnp.zeros((length, length), F32)
         for j in range(2):
-            g_j = (gf * sel[j]).astype(BF16)
             size = rdt[c, j : j + 1, :]
-            k1 = decs[c, j] * mm(g_j, xs, 1, 1)
+            k1 = decs[c, j] * mm((gf * sel[j]).astype(BF16), xs, 1, 1)
             k0 = k1 * aff
             ds0[c, j : j + 1, :] = jnp.sum(k0, axis=0, keepdims=True)
             crossing = mm((k0 * size).astype(BF16), before.astype(BF16), 1, 0)
@@ -415,84 +500,70 @@
                 jnp.where(causal, crossing, 0.0), axis=0, keepdims=True
             )
             pulls = pulls + k1 * size
-            dx_sum = dx_sum + mm(scores[c, j], g_j, 0, 0)
         pulls = pulls.astype(BF16)
-        dx_in[c] = dx_sum
-        sdc[c] = (mm(pulls, bs, 1, 0) + mm(eg[c], hb[c], 1, 1)).astype(BF16)
-        db_in[c] = mm(pulls, cs, 0, 0)
+        dc_in[c] = mm(pulls, rb[c], 1, 0)
+        db_in[c] = mm(pulls, rc[c], 0, 0)
         skipsum[pl.ds(c, 1), :] = jnp.sum(xf * gf, axis=0, keepdims=True)
-
-    def leave_c(k):
-        c = lax.rem(r + k, row)
-
-        @pl.when(k == 0)
-        def _():
-            keep(sdc.at[c], rdc.at[r], dc_recv.at[r])
-
-        @pl.when(k > 0)
-        def _():
-            send(sdc.at[c], rdc.at[r], dc_send, dc_recv.at[r], at(c, z))
-
-    pairs(row, pulled, leave_c)
-
-    back = jnp.zeros((STATE, LANES), F32)
-    for i in reversed(range(1, slabs)):
-        source = lax.rem(y + i, slabs)
-
-        @pl.when(y + i < slabs)
-        def _():
-            bytes_wait(arecv.at[source], a_recv.at[source])
-
-        fade, part = rkept[source, 0:1], arecv[source].astype(F32)
-        back = jnp.where(y + i < slabs, fade * back + part, back)
-    for c in reversed(range(row)):
-        hb[c] = back.astype(BF16)
-        fade = last_decay(c)
-        over = fade * jnp.sum(st_s[c] * back, axis=0, keepdims=True)
+        then(c)
+
+    def added(landing, recv_sem):
+        loop(0, half, lambda c: bytes_wait(landing.at[c], recv_sem.at[c]))
+        total = landing[0].astype(F32)
+        for c in range(1, half):
+            total = total + landing[c].astype(F32)
+        return total.astype(BF16)
+
+    def send_oc(i):
+        to = lax.rem(z + i, zs)
+        send(szc.at[tokens_of(to), :], rzc.at[z], oc_send, oc_recv, at(r, to))
+
+    def small_out(landing, recv_sem):
+        szc[...] = added(landing, recv_sem)
+        keep(szc.at[mine, :], rzc.at[z], oc_recv)
+        loop(1, zs, send_oc)
+
+    def both(k, one, two):
+        one(k)
+        two(k)
+
+    def x_first():
+        states_out()
+        loop(0, row, lambda c: bytes_wait(rc.at[c], c_recv.at[c]))
+        pairs(row, functools.partial(scored, inner_y))
+        cotangents_late()
+        await_kept()
+        states_in()
+        pairs(row, finish_y, leave_y)
+        pairs(row, functools.partial(pulled, inner_x))
+        pairs(row, finish_c)
+        c_to_mate()
+        cotangents_in()
+        c_to_chips()
+        pairs(row, lambda k: both(k, finish_x, finish_b))
+        b_to_mate()
+
+    def g_first():
+        cotangents_out()
+        loop(0, row, lambda c: bytes_wait(rb.at[c], b_recv.at[c]))
+        pairs(row, functools.partial(scored, inner_x))
+        states_late()
+        await_kept()
+        cotangents_in()
+        pairs(row, finish_x, leave_x)
+        pairs(row, functools.partial(pulled, inner_y))
+        pairs(row, finish_b)
+        b_to_mate()
+        states_in()
+        b_to_chips()
+        pairs(row, lambda k: both(k, finish_y, finish_c))
+        c_to_mate()
+
+    either(x_first, g_first)
+    for c in range(row):
+        over = last_decay(c) * jnp.sum(st_s[c] * st_a[c], axis=0, keepdims=True)
         cterm[c] = jnp.broadcast_to(
             jnp.sum(pick[0:8] * over, axis=1, keepdims=True), (8, length)
         )
-        back = fade * back + st_a[c]
-
-    def finish_x(k):
-        c = lax.rem(r + k, row)
-        bi = wcol[c] * mm(rb[c], hb[c], 1, 0)
-        sdx[c] = (dx_in[c] + bi).astype(BF16)
-        sdb[c] = (db_in[c] + mm(wx[c], hb[c], 1, 1)).astype(BF16)
-        kap[c] = mm(pick16, (rx[c].astype(F32) * bi).astype(BF16), 1, 1)[0:8]
-
-    def leave_x(k):
-        leave(sdx, k, lax.rem(r + k, row), rdx, dx_send, dx_recv)
-
-    def leave_b(k):
-        c = lax.rem(r + k, row)
-
-        @pl.when(k == 0)
-        def _():
-            keep(sdb.at[c], rdb.at[r], db_recv.at[r])
-
-        @pl.when(k > 0)
-        def _():
-            send(sdb.at[c], rdb.at[r], db_send, db_recv.at[r], at(c, z))
-
-        @pl.when(k < FIRST)
-        def _():
-            leave_x(k)
-
-    pairs(row, finish_x, leave_b)
-
-    loop(0, row, lambda c: bytes_wait(rdc.at[c], dc_recv.at[c]))
-    total = rdc[0].astype(F32)
-    for c in range(1, row):
-        total = total + rdc[c].astype(F32)
-    szc[...] = total.astype(BF16)
-    keep(szc.at[mine, :], rzc.at[z], oc_recv)
-
-    def send_oc(i):
-        to = lax.rem(z + i, zs)
-        send(szc.at[tokens_of(to), :], rzc.at[z], oc_send, oc_recv, at(r, to))
-
-    loop(1, zs, send_oc)
 
     flat = (row * 8, length)
     dla = (
@@ -538,13 +609,23 @@
         send(ssy, rsy.at[y], sy_send, sy_recv, (lax.rem(y + i, slabs) * row + r, z))
 
     loop(1, slabs, send_sy)
-    loop(FIRST, row, leave_x)
-
-    loop(0, row, lambda c: bytes_wait(rdb.at[c], db_recv.at[c]))
-    total = rdb[0].astype(F32)
-    for c in range(1, row):
-        total = total + rdb[c].astype(F32)
-    szo[0] = total.astype(BF16)
+
+    def x_out():
+        loop(0, row, leave_x)
+        b_to_chips()
+        small_out(rdc, dc_recv)
+
+    def y_out():
+        loop(0, row, leave_y)
+        c_to_chips()
+        small_out(rdb, db_recv)
+
+    either(x_out, y_out)
+
+    def late_sum(landing, recv_sem):
+        szo[0] = added(landing, recv_sem)
+
+    either(lambda: late_sum(rdb, db_recv), lambda: late_sum(rdc, dc_recv))
     loop(0, row, lambda c: bytes_wait(rgd.at[c], gd_recv.at[c]))
     turn[...] = jnp.zeros_like(turn)
     turn[pl.ds(pl.multiple_of(z * per, per), per), :] = jnp.concatenate(
@@ -571,33 +652,64 @@
 
     loop(1, row, send_sr)
 
-    bytes_wait(ry, y_recv)
+    results = [
+        pltpu.make_async_copy(inner_ref.at[0], inner_hbm.at[0], done.at[0]),
+        pltpu.make_async_copy(inner_ref.at[1], inner_hbm.at[1], done.at[1]),
+        pltpu.make_async_copy(outer_ref, outer_hbm, done.at[2]),
+        pltpu.make_async_copy(gdt_ref, gdt_hbm, done.at[3]),
+        pltpu.make_async_copy(sums_ref, sums_hbm, done.at[4]),
+    ]
 
     def gate_back(k):
         for i in range(row):
             d = k * row + i
             inner_ref[1, :, lanes_of(d)] = (slope[d] * ry[d].astype(F32)).astype(BF16)
 
-    loop(0, zs, gate_back)
-    bytes_wait(rzc, oc_recv)
-    for k in range(zs):
-        outer_ref[1, :, k * STATE : (k + 1) * STATE] = rzc[k]
-    bytes_wait(rdx, dx_recv)
-    for d in range(row * zs):
-        inner_ref[0, :, d * LANES : (d + 1) * LANES] = rdx[d]
-
-    bytes_wait(rzo, zo_recv)
+    def take_y():
+        bytes_wait(ry, y_recv)
+        loop(0, zs, gate_back)
+        results[1].start()
+
+    def take_x():
+        bytes_wait(rdx, dx_recv)
+        for d in range(row * zs):
+            inner_ref[0, :, d * LANES : (d + 1) * LANES] = rdx[d]
+        results[0].start()
+
+    def take_small(early, late):
+        bytes_wait(rzc, oc_recv)
+        for k in range(zs):
+            outer_ref[early, :, k * STATE : (k + 1) * STATE] = rzc[k]
+        bytes_wait(rzo, zo_recv)
+        for k in range(zs):
+            outer_ref[late, :, k * STATE : (k + 1) * STATE] = rzo[k, 0]
+
+    def x_last():
+        take_y()
+        take_x()
+        take_small(1, 0)
+
+    def y_last():
+        take_x()
+        take_y()
+        take_small(0, 1)
+
+    either(x_last, y_last)
     total = jnp.zeros((TOK, heads), F32)
     for k in range(zs):
-        outer_ref[0, :, k * STATE : (k + 1) * STATE] = rzo[k, 0]
         total = total + rzo[k, 1, :, 0:heads].astype(F32)
     gdt_ref[...] = total.astype(BF16)
+    results[2].start()
+    results[3].start()
     bytes_wait(rsr, sr_recv)
     total = rsr[0]
     for i in range(1, row):
         total = total + rsr[i]
     sums_ref[...] = total
-
+    results[4].start()
+
+    for copy in results:
+        copy.wait()
     @pl.when(y < slabs - 1)
     def _():
         loop(0, slabs - 1 - y, lambda i: bytes_wait(ssend, s_send))
@@ -615,8 +727,11 @@
     bytes_wait(rb.at[others], b_send)
     bytes_wait(rc.at[others], c_send)
     bytes_wait(sdt.at[others], dt_send)
-    bytes_wait(rdb.at[others], db_send)
-    bytes_wait(rdc.at[others], dc_send)
+    chips = pl.ds(0, half - 1)
+    bytes_wait(rdb.at[chips], db_send)
+    bytes_wait(rdc.at[chips], dc_send)
+    bytes_wait(mdb, mb_send)
+    bytes_wait(mdc, mc_send)
     bytes_wait(sgd.at[others], gd_send)
     bytes_wait(rzo.at[pl.ds(0, zs - 1)], zo_send)
     bytes_wait(rzc.at[pl.ds(0, zs - 1)], oc_send)
@@ -626,24 +741,34 @@
 
 
 def unpack(
-    inner_hbm, outer_hbm, dt_hbm, sums_ref,
+    inner_hbm, outer_hbm, dt_hbm, sums_hbm,
     gx_ref, gz_ref, gb_ref, gc_ref, gdt_ref, bias_ref, alog_ref, skip_ref,
-    inner, outer, dts, come, go,
+    inner, outer, dts, sums, bias, alog, skip, come, go,
 ):
-    moves = (
-        (inner_hbm.at[0], inner.at[0], gx_ref),
-        (inner_hbm.at[1], inner.at[1], gz_ref),
+    width = gx_ref.shape[1] // PARTS
+    moves = []
+    for q, ref in enumerate((gx_ref, gz_ref)):
+        for p in range(PARTS):
+            part = pl.ds(p * width, width)
+            moves.append((inner_hbm.at[q, :, part], inner.at[q, :, part], ref.at[:, part]))
+    moves += [
         (outer_hbm.at[0], outer.at[0], gb_ref),
         (outer_hbm.at[1], outer.at[1], gc_ref),
         (dt_hbm, dts, gdt_ref),
-    )
+    ]
     came = [pltpu.make_async_copy(a, b, come.at[i]) for i, (a, b, _) in enumerate(moves)]
     gone = [pltpu.make_async_copy(b, c, go.at[i]) for i, (_, b, c) in enumerate(moves)]
+    last = len(moves)
+    came_sums = pltpu.make_async_copy(sums_hbm, sums, come.at[last])
+    came_sums.start()
     for copy in came:
         copy.start()
-    for q, ref in enumerate((bias_ref, alog_ref, skip_ref)):
-        ref[...] = sums_ref[q, 0 : ref.shape[0]]
-    for first, second in zip(came, gone):
+    came_sums.wait()
+    for q, (row, ref) in enumerate(((bias, bias_ref), (alog, alog_ref), (skip, skip_ref))):
+        row[...] = sums[q, 0 : row.shape[0]]
+        gone.append(pltpu.make_async_copy(row, ref, go.at[last + q]))
+        gone[-1].start()
+    for first, second in zip(came, gone[:last]):
         first.wait()
         second.start()
     for copy in gone:
@@ -661,6 +786,7 @@
         return pltpu.VMEM(shape, dtype)
 
     square = (row, length, LANES)
+    half = (row // 2, length, LANES)
     states = (row, STATE, LANES)
     per = 2 * row
     scratch = [
@@ -698,8 +824,12 @@
         vmem(row * zs, TOK, LANES),
         vmem(*square),
         vmem(*square),
-        vmem(*square),
-        vmem(*square),
+        vmem(*half),
+        vmem(*half),
+        vmem(*half),
+        vmem(*half),
+        vmem(*half),
+        vmem(*half),
         vmem(row, 8, length, dtype=F32),
         vmem(row, 8, length, dtype=F32),
         vmem(2, length, STATE),
@@ -710,6 +840,10 @@
         vmem(slabs, 8, LANES, dtype=F32),
         vmem(8, LANES, dtype=F32),
         vmem(row, 8, LANES, dtype=F32),
+        vmem(2, TOK, inner),
+        vmem(2, TOK, zs * STATE),
+        vmem(TOK, heads),
+        vmem(8, LANES, dtype=F32),
         vmem(row * zs, TOK, LANES, dtype=F32),
         vmem(heads, length, dtype=F32),
         vmem(row, length, 8, dtype=F32),
@@ -720,9 +854,11 @@
         vmem(*states, dtype=F32),
         vmem(*states, dtype=F32),
         vmem(*states),
+        vmem(*states),
         vmem(row, length, length, dtype=F32),
         vmem(row, 2, length, length, dtype=F32),
         vmem(row, 2, length, length),
+        vmem(*square, dtype=F32),
         vmem(*square, dtype=F32),
         vmem(*square, dtype=F32),
         vmem(*square, dtype=F32),
@@ -747,16 +883,18 @@
         one, many(slabs),
         one, one,
         one, one,
-        one, many(row),
-        one, many(row),
+        one, many(row // 2),
+        one, many(row // 2),
+        one, many(row // 2),
+        one, many(row // 2),
         one, many(row),
         one, one,
         one, one,
         one, one,
         one, one,
         many(9),
+        many(5),
     ]
-    in_vmem = pl.BlockSpec(memory_space=pltpu.VMEM)
     in_hbm = pl.BlockSpec(memory_space=pltpu.HBM)
     like = jax.ShapeDtypeStruct
     results = pl.pallas_call(
@@ -768,7 +906,7 @@
             like((8, LANES), F32),
         ],
         in_specs=[in_hbm] * 9,
-        out_specs=[in_vmem] * 4,
+        out_specs=[in_hbm] * 4,
         scratch_shapes=scratch + semaphores,
         compiler_params=pltpu.CompilerParams(
             collective_id=0, has_side_effects=True, vmem_limit_bytes=62 * 2**20
@@ -788,14 +926,18 @@
             like((per,), F32),
             like((per,), F32),
         ],
-        in_specs=[anywhere] * 3 + [in_vmem],
-        out_specs=[anywhere] * 5 + [in_vmem] * 3,
+        in_specs=[anywhere] * 4,
+        out_specs=[anywhere] * 8,
         scratch_shapes=[
             vmem(2, TOK, inner),
             vmem(2, TOK, zs * STATE),
             vmem(TOK, heads),
-            many(5),
-            many(5),
+            vmem(8, LANES, dtype=F32),
+            vmem(per, dtype=F32),
+            vmem(per, dtype=F32),
+            vmem(per, dtype=F32),
+            many(2 * PARTS + 4),
+            many(2 * PARTS + 6),
         ],
         compiler_params=pltpu.CompilerParams(vmem_limit_bytes=62 * 2**20),
         name="unpack",

time: 65.3 us -> 62.1 us (0.951)
  the two profiles are of different devices: /device:TPU:1 before, /device:TPU:24 now
where the time goes in v4:
time: 62.1 us; the launch traced here: 61.9 us
  Pallas kernels  61.3 us (99%)
  between operations  0.64 us (1%)
    pallas_call x1, Pallas kernels, shards(): pl.pallas_call(functools.partial(kernel, (slabs, row, zs, heads)), out_sh...  59.3 us
    pallas_call x1, Pallas kernels, shards(): pl.pallas_call(unpack, out_shape=[like((TOK, inner), BF16), like((TOK, in...  1.95 us

profile of v4, /device:TPU:24, one launch (start us, length us, event | category | flops | bytes accessed | tf_op | source)
XLA Modules:
  0.0 61.9 jit_solution(17706362636007506271)
XLA Ops:
  0.6 59.3 %scan_backward.1 = (bf16[2,16,8192]{2,1,0:T(8,128)(2,1)}, bf16[2,16,1024]{2,1,0:T(8,128)(2,1)}, bf16[16,128]{1,0:T(8,128)(2,1)}, f32[8,128]{1,0:T(8,128)}) custom-call(bf16[16,8192]{1,0:T(8,128)(2,1)} %x_hbm.1, bf16[16,8192]{1,0:T(8,128)(2,1)} %z_hbm.1, bf16[16,8192]{1,0:T(8,128)(2,1)} %og_hbm.1, bf16[16,1024]{1,0:T(8,128)(2,1)} %b_hbm.1, ...), custom_call_target="tpu_custom_call" | custom-call | tf_op jit(solution)/shard_map/scan_backward/pallas_call | solution.py:900
  60.0 2.0 %unpack.1 = (bf16[16,8192]{1,0:T(8,128)(2,1)}, bf16[16,8192]{1,0:T(8,128)(2,1)}, bf16[16,1024]{1,0:T(8,128)(2,1)}, bf16[16,1024]{1,0:T(8,128)(2,1)}, bf16[16,128...) custom-call(bf16[2,16,8192]{2,1,0:T(8,128)(2,1)} %get-tuple-element.12.inner_hbm, ...), custom_call_target="tpu_custom_call" | custom-call | tf_op jit(solution)/shard_map/unpack/pallas_call | solution.py:917

commit v5 on v4

--- a/solution.py
+++ b/solution.py
@@ -611,13 +611,15 @@
     loop(1, slabs, send_sy)
 
     def x_out():
-        loop(0, row, leave_x)
+        loop(0, row // 2, leave_x)
         b_to_chips()
+        loop(row // 2, row, leave_x)
         small_out(rdc, dc_recv)
 
     def y_out():
-        loop(0, row, leave_y)
+        loop(0, row // 2, leave_y)
         c_to_chips()
+        loop(row // 2, row, leave_y)
         small_out(rdb, db_recv)
 
     either(x_out, y_out)

time: 62.1 us -> 61.2 us (0.986)
  the two profiles are of different devices: /device:TPU:24 before, /device:TPU:1 now
where the time goes in v5:
time: 61.2 us; the launch traced here: 60.8 us
  Pallas kernels  60.1 us (98%)
  between operations  0.64 us (1%)
    pallas_call x1, Pallas kernels, shards(): pl.pallas_call(functools.partial(kernel, (slabs, row, zs, heads)), out_sh...  58.2 us
    pallas_call x1, Pallas kernels, shards(): pl.pallas_call(unpack, out_shape=[like((TOK, inner), BF16), like((TOK, in...  1.95 us

profile of v5, /device:TPU:1, one launch (start us, length us, event | category | flops | bytes accessed | tf_op | source)
XLA Modules:
  0.0 60.8 jit_solution(14381513745875260673)
XLA Ops:
  0.6 58.2 %scan_backward.1 = (bf16[2,16,8192]{2,1,0:T(8,128)(2,1)}, bf16[2,16,1024]{2,1,0:T(8,128)(2,1)}, bf16[16,128]{1,0:T(8,128)(2,1)}, f32[8,128]{1,0:T(8,128)}) custom-call(bf16[16,8192]{1,0:T(8,128)(2,1)} %x_hbm.1, bf16[16,8192]{1,0:T(8,128)(2,1)} %z_hbm.1, bf16[16,8192]{1,0:T(8,128)(2,1)} %og_hbm.1, bf16[16,1024]{1,0:T(8,128)(2,1)} %b_hbm.1, ...), custom_call_target="tpu_custom_call" | custom-call | tf_op jit(solution)/shard_map/scan_backward/pallas_call | solution.py:902
  58.8 2.0 %unpack.1 = (bf16[16,8192]{1,0:T(8,128)(2,1)}, bf16[16,8192]{1,0:T(8,128)(2,1)}, bf16[16,1024]{1,0:T(8,128)(2,1)}, bf16[16,1024]{1,0:T(8,128)(2,1)}, bf16[16,128...) custom-call(bf16[2,16,8192]{2,1,0:T(8,128)(2,1)} %get-tuple-element.12.inner_hbm, ...), custom_call_target="tpu_custom_call" | custom-call | tf_op jit(solution)/shard_map/unpack/pallas_call | solution.py:919
